TPU v7x, 32 devices: a whole 2x2x4 slice. The times are simulated.
32 devices in a mesh: fsdp: 8 (over z, y), rep: 4 (over x, core).
Axes of the slice: x: 2, y: 2, z: 4, core: 2. Of those that a mesh axis runs over, the one named last changes fastest.
Arguments:
- tokens: bfloat16 [2, 4096, 2048], P(None, ('fsdp', 'rep')), may hold values from -6 to 6
- segment_ids: int32 [2, 32, 128], P(None, ('fsdp', 'rep')), may hold values from 0 to 2, never falling along the last dimension, each value on 1 to 64 neighbouring positions
- out_grad: bfloat16 [2, 4096, 2048], P(None, ('fsdp', 'rep')), may hold values from -6 to 6
- norm_gain: bfloat16 [2048], P('fsdp'), may hold values from 0.25 to 1.75
- in_proj: bfloat16 [2048, 8192], P('fsdp'), may hold values from -0.125 to 0.125
- conv_weight: bfloat16 [4096, 4], P('fsdp'), may hold values from -3 to 3
- conv_bias: bfloat16 [4096], P('fsdp'), may hold values from -3 to 3
- x_proj: bfloat16 [4096, 160], P('fsdp'), may hold values from -0.09375 to 0.09375
- step_proj: bfloat16 [4096, 128], P('fsdp'), may hold values from -0.5 to 0.5
- step_bias: bfloat16 [4096], P('fsdp'), may hold values from -4 to -1
- decay_log: bfloat16 [4096, 16], P('fsdp'), may hold values from -1 to 2.5
- skip_gain: bfloat16 [4096], P('fsdp'), may hold values from 0.5 to 1.5
- out_proj: bfloat16 [4096, 2048], P('fsdp'), may hold values from -0.375 to 0.375
Outputs:
- block_out: bfloat16 [2, 4096, 2048], P(None, ('fsdp', 'rep'))
- input_grad: bfloat16 [2, 4096, 2048], P(None, ('fsdp', 'rep'))
- gain_grad: float32 [2048], P('fsdp')
- in_proj_grad: float32 [2048, 8192], P('fsdp')
- conv_weight_grad: float32 [4096, 4], P('fsdp')
- conv_bias_grad: float32 [4096], P('fsdp')
- x_proj_grad: float32 [4096, 160], P('fsdp')
- step_proj_grad: float32 [4096, 128], P('fsdp')
- step_bias_grad: float32 [4096], P('fsdp')
- decay_log_grad: float32 [4096, 16], P('fsdp')
- skip_gain_grad: float32 [4096], P('fsdp')
- out_proj_grad: float32 [4096, 2048], P('fsdp')
Inputs may be any that keep to these rules, and one draw needn't show every extreme that they name: `segment_ids`: segment numbers never fall along a sequence; each change starts a new document.
All inputs are finite; a program needn't handle non-finite values.
Results may differ from a plain program's by a relative error of at most 0.012.
Values may be sent and summed in bfloat16 or wider, within the bound.
A program may use at most 240 MiB of HBM per device.

v0:
```python
import functools

import jax
import jax.numpy as jnp
from jax import lax
from jax.experimental import pallas as pl
from jax.experimental.pallas import tpu as pltpu
from jax.sharding import PartitionSpec as P

EPS = 1e-05
BLOCK = 16
LANES = 128
GROUP = 8
COPIES = 4
LOG2E = 1.4426950408889634
LN2 = 0.6931471805599453
FAR = 1e30
F32 = jnp.float32
BF16 = jnp.bfloat16
VMEM_LIMIT = 56 * 1024 * 1024


def dot(left, right, left_dim, right_dim):
    return lax.dot_general(
        left, right, (((left_dim,), (right_dim,)), ((), ())), preferred_element_type=F32
    )


def params():
    return pltpu.CompilerParams(vmem_limit_bytes=VMEM_LIMIT)


def cost(flops, moved):
    return pl.CostEstimate(flops=int(flops), bytes_accessed=int(moved), transcendentals=0)


def blank(shape, dtype):
    return pl.pallas_call(
        lambda ref: None,
        out_shape=jax.ShapeDtypeStruct(shape, dtype),
        out_specs=pl.BlockSpec(memory_space=pl.ANY),
        name="blank",
    )()


def ring_order(size):
    half = size // 2
    return [2 * p if p < half else 2 * (size - 1 - p) + 1 for p in range(size)]


class Ring:
    def __init__(self, size):
        order = ring_order(size)
        place = [0] * size
        for spot, member in enumerate(order):
            place[member] = spot
        self.size, self.half = size, size // 2
        self.order = jnp.array(order, jnp.int32)
        self.spot = jnp.array(place, jnp.int32)[lax.axis_index("fsdp")]
        self.above = [(order[p], order[(p + 1) % size]) for p in range(size)]
        self.below = [(order[p], order[(p - 1) % size]) for p in range(size)]

    def member(self, offset):
        return self.order[(self.spot + offset + self.size) % self.size]

    def up(self, value):
        return lax.ppermute(value, "fsdp", self.above)

    def down(self, value):
        return lax.ppermute(value, "fsdp", self.below)


class Gather:
    def __init__(self, ring, shard):
        self.ring, self.cut = ring, shard.shape[0] // 2
        self.whole = blank((ring.size,) + shard.shape, shard.dtype)
        self.held = (shard, shard)
        self.put(shard, 0)

    def put(self, piece, offset, start=0):
        at = (self.ring.member(offset), jnp.int32(start), jnp.int32(0))
        self.whole = lax.dynamic_update_slice(self.whole, piece[None], at)

    def step(self, number):
        low, high = self.held
        if number == self.ring.half:
            low, high = low[: self.cut], high[self.cut :]
        return self.ring.up(low), self.ring.down(high)

    def take(self, number, got):
        self.held = got
        last = number == self.ring.half
        self.put(got[0], -number)
        self.put(got[1], number, self.cut if last else 0)

    def rest(self):
        def body(number, state):
            whole, low, high = state
            low, high = self.ring.up(low), self.ring.down(high)
            self.whole = whole
            self.put(low, -number)
            self.put(high, number)
            return self.whole, low, high

        self.whole, low, high = lax.fori_loop(1, self.ring.half, body, (self.whole,) + self.held)
        self.held = (low, high)
        self.take(self.ring.half, self.step(self.ring.half))


class Scatter:
    def __init__(self, ring, parts):
        self.ring, self.parts, self.cut = ring, parts, parts.shape[1] // 2
        far = self.own(ring.half)
        self.sent = (far[: self.cut], far[self.cut :])
        self.total = None

    def own(self, offset):
        return lax.dynamic_index_in_dim(self.parts, self.ring.member(offset), 0, keepdims=False)

    def step(self, number):
        return self.ring.up(self.sent[0]), self.ring.down(self.sent[1])

    def take(self, number, got):
        left = self.ring.half - number
        low, high = got
        near_low, near_high = self.own(left), self.own(-left)
        if number == 1:
            low = jnp.concatenate([low, jnp.zeros_like(near_low[self.cut :])])
            high = jnp.concatenate([jnp.zeros_like(near_high[: self.cut]), high])
        if left == 0:
            self.total = near_low.astype(F32) + low.astype(F32) + high.astype(F32)
        else:
            self.sent = (self.add(near_low, low), self.add(near_high, high))

    def add(self, near, got):
        return (near.astype(F32) + got.astype(F32)).astype(near.dtype)

    def rest(self):
        self.take(1, self.step(1))

        def body(number, sent):
            left = self.ring.half - number
            low, high = self.ring.up(sent[0]), self.ring.down(sent[1])
            return self.add(self.own(left), low), self.add(self.own(-left), high)

        self.sent = lax.fori_loop(2, self.ring.half, body, self.sent)
        self.take(self.ring.half, self.step(self.ring.half))


def after(value, *held):
    return lax.optimization_barrier((value, held))[1]


def slot(number, movers, *work):
    moved = tuple(m.step(number) for m in movers)
    done = tuple(w() for w in work)
    moved, done = lax.optimization_barrier((moved, done))
    for mover, got in zip(movers, moved):
        mover.take(number, got)
    return done


def swap(value, bit):
    return lax.ppermute(value, "rep", [(r, r ^ bit) for r in range(COPIES)])


def rep_gather(value):
    across = swap(value, 2)
    return [value, swap(value, 1), across, swap(across, 1)]


def rep_scatter_near(parts):
    pair = swap(jnp.stack([parts[1], parts[3]]), 1)
    near = parts[0].astype(F32) + pair[0].astype(F32)
    far = parts[2].astype(F32) + pair[1].astype(F32)
    return near, far.astype(parts.dtype)


def rep_scatter_far(near, far):
    return near + swap(far, 2).astype(F32)


def sum_near(parts):
    pair = swap(jnp.stack([parts[1], parts[3]]), 1)
    mine = jnp.stack([parts[0], parts[2]]) + pair
    return mine + swap(jnp.stack([mine[1], mine[0]]), 2)


def sum_far(mine):
    next_to = swap(mine, 1)
    return jnp.stack([mine[0], next_to[0], mine[1], next_to[1]])


def to_time(value):
    return jnp.swapaxes(value.reshape(GROUP, -1, value.shape[-1]), 0, 1).reshape(value.shape)


def to_sequence(value):
    return jnp.swapaxes(value.reshape(-1, GROUP, value.shape[-1]), 0, 1).reshape(value.shape)


def by_copy(value):
    return value.reshape(COPIES, -1, value.shape[-1])


def sigmoid(value):
    return 1.0 / (1.0 + jnp.exp(-value))


def later(value, shift):
    rows = shift * GROUP
    return jnp.concatenate([jnp.zeros_like(value[:rows]), value[:-rows]], axis=0)


def sooner(value, shift):
    rows = shift * GROUP
    return jnp.concatenate([value[rows:], jnp.zeros_like(value[:rows])], axis=0)


def conv_of(inner, masks, taps):
    total = taps[4:5] + taps[3:4] * inner
    for shift in range(1, 4):
        total = total + taps[3 - shift : 4 - shift] * (later(inner, shift) * masks[shift - 1])
    return total


def by_sequence(held, out_ref, value):
    length = value.shape[0] // GROUP
    held[...] = value
    for s in range(GROUP):
        out_ref[s * length : (s + 1) * length, :] = held[
            pl.ds(s, length, stride=GROUP), :
        ].astype(out_ref.dtype)


def conv_kernel(inner_ref, masks_ref, taps_ref, act_ref, low_ref, held):
    value = conv_of(inner_ref[...], masks_ref, taps_ref[...])
    act = value * sigmoid(value)
    act_ref[...] = act
    by_sequence(held, low_ref, act)


def conv_forward(inner, masks, taps):
    rows, width = inner.shape
    tile = pl.BlockSpec((rows, LANES), lambda c: (0, c))
    return pl.pallas_call(
        conv_kernel,
        grid=(width // LANES,),
        in_specs=[
            tile,
            pl.BlockSpec((3, rows, LANES), lambda c: (0, 0, 0)),
            pl.BlockSpec((8, LANES), lambda c: (0, c)),
        ],
        out_specs=[tile, tile],
        out_shape=[
            jax.ShapeDtypeStruct((rows, width), F32),
            jax.ShapeDtypeStruct((rows, width), BF16),
        ],
        scratch_shapes=[pltpu.VMEM((rows, LANES), F32)],
        compiler_params=params(),
        cost_estimate=cost(30 * rows * width, 10 * rows * width),
        name="conv_forward",
    )(inner, masks, taps)


def conv_back_kernel(inner_ref, grad_ref, masks_ref, taps_ref, out_ref, natural_ref, sums_ref, held):
    inner, taps = inner_ref[...], taps_ref[...]
    value = conv_of(inner, masks_ref, taps)
    gate = sigmoid(value)
    grad = grad_ref[...] * (gate * (1.0 + value * (1.0 - gate)))
    total = taps[3:4] * grad
    sums = [None] * 4 + [jnp.sum(grad, axis=0, keepdims=True)]
    sums[3] = jnp.sum(grad * inner, axis=0, keepdims=True)
    for shift in range(1, 4):
        masked = grad * masks_ref[shift - 1]
        total = total + taps[3 - shift : 4 - shift] * sooner(masked, shift)
        sums[3 - shift] = jnp.sum(masked * later(inner, shift), axis=0, keepdims=True)
    out_ref[...] = total.astype(BF16)
    by_sequence(held, natural_ref, total)
    sums_ref[...] = jnp.concatenate(sums + [jnp.zeros((3, inner.shape[1]), F32)], axis=0)


def conv_backward(inner, grad, masks, taps):
    rows, width = inner.shape
    tile = pl.BlockSpec((rows, LANES), lambda c: (0, c))
    few = pl.BlockSpec((8, LANES), lambda c: (0, c))
    return pl.pallas_call(
        conv_back_kernel,
        grid=(width // LANES,),
        in_specs=[tile, tile, pl.BlockSpec((3, rows, LANES), lambda c: (0, 0, 0)), few],
        out_specs=[tile, tile, few],
        out_shape=[
            jax.ShapeDtypeStruct((rows, width), BF16),
            jax.ShapeDtypeStruct((rows, width), BF16),
            jax.ShapeDtypeStruct((8, width), F32),
        ],
        scratch_shapes=[pltpu.VMEM((rows, LANES), F32)],
        compiler_params=params(),
        cost_estimate=cost(60 * rows * width, 10 * rows * width),
        name="conv_backward",
    )(inner, grad, masks, taps)


def gate_kernel(readout_ref, gate_ref, out_ref, natural_ref, held):
    gate = gate_ref[...]
    gated = readout_ref[...] * (gate * sigmoid(gate))
    out_ref[...] = gated.astype(BF16)
    by_sequence(held, natural_ref, gated)


def gate_forward(readout, gate):
    rows, width = gate.shape
    tile = pl.BlockSpec((rows, LANES), lambda c: (0, c))
    return pl.pallas_call(
        gate_kernel,
        grid=(width // LANES,),
        in_specs=[tile] * 2,
        out_specs=[tile] * 2,
        out_shape=[jax.ShapeDtypeStruct((rows, width), BF16)] * 2,
        scratch_shapes=[pltpu.VMEM((rows, LANES), F32)],
        compiler_params=params(),
        cost_estimate=cost(20 * rows * width, 12 * rows * width),
        name="gate_forward",
    )(readout, gate)


def gate_back_kernel(grad_ref, readout_ref, gate_ref, read_ref, out_ref, natural_ref, held):
    gate, grad = gate_ref[...], grad_ref[...]
    sig = sigmoid(gate)
    read_ref[...] = grad * (gate * sig)
    gate_grad = grad * readout_ref[...] * (sig * (1.0 + gate * (1.0 - sig)))
    out_ref[...] = gate_grad.astype(BF16)
    by_sequence(held, natural_ref, gate_grad)


def gate_backward(grad, readout, gate):
    rows, width = gate.shape
    tile = pl.BlockSpec((rows, LANES), lambda c: (0, c))
    return pl.pallas_call(
        gate_back_kernel,
        grid=(width // LANES,),
        in_specs=[tile] * 3,
        out_specs=[tile] * 3,
        out_shape=[jax.ShapeDtypeStruct((rows, width), F32)]
        + [jax.ShapeDtypeStruct((rows, width), BF16)] * 2,
        scratch_shapes=[pltpu.VMEM((rows, LANES), F32)],
        compiler_params=params(),
        cost_estimate=cost(20 * rows * width, 20 * rows * width),
        name="gate_backward",
    )(grad, readout, gate)


def rows_kernel(scaled, *refs):
    values_ref, out_ref, held = refs[0], refs[-2], refs[-1]
    for s in range(GROUP):
        value = values_ref[s].astype(F32)
        if scaled:
            square = jnp.mean(value * value, axis=-1, keepdims=True)
            value = value * lax.rsqrt(square + EPS) * refs[1][...]
        for k in range(held.shape[0]):
            held[k, pl.ds(s, value.shape[0], stride=GROUP), :] = value[
                :, k * LANES : (k + 1) * LANES
            ]
    for k in range(held.shape[0]):
        out_ref[:, k * LANES : (k + 1) * LANES] = held[k].astype(BF16)


def interleave(values, gain=None):
    _, length, model = values.shape
    extra = [] if gain is None else [gain.reshape(1, model)]
    return pl.pallas_call(
        functools.partial(rows_kernel, gain is not None),
        grid=(length // BLOCK,),
        in_specs=[pl.BlockSpec((GROUP, BLOCK, model), lambda t: (0, t, 0))]
        + [pl.BlockSpec((1, model), lambda t: (0, 0))] * len(extra),
        out_specs=pl.BlockSpec((BLOCK * GROUP, model), lambda t: (t, 0)),
        out_shape=jax.ShapeDtypeStruct((length * GROUP, model), BF16),
        scratch_shapes=[pltpu.VMEM((model // LANES, BLOCK * GROUP, LANES), F32)],
        compiler_params=params(),
        cost_estimate=cost(8 * GROUP * length * model, 4 * GROUP * length * model),
        name="interleave",
    )(values, *extra)


class Peers:
    def __init__(self, size):
        self.size, self.half = size, size // 2
        self.member, self.copy = lax.axis_index("fsdp"), lax.axis_index("rep")
        row, column = lax.div(self.member, 2), lax.rem(self.member, 2)
        self.spot = row * (1 - column) + (size - 1 - row) * column
        side = lax.rem(self.copy, 2)
        self.core = (self.member, self.copy - side + (1 - side))
        self.across = (self.member, lax.rem(self.copy + 2, COPIES))
        self.ring = ((self.at(1), self.copy), (self.at(-1), self.copy))

    def at(self, offset):
        spot = lax.rem(self.spot + (offset + self.size), self.size)
        second = lax.div(spot, self.half)
        return 2 * spot * (1 - second) + (2 * (self.size - 1 - spot) + 1) * second

    def meet(self):
        barrier = pltpu.get_barrier_semaphore()
        peers = (*self.ring, self.core, self.across)
        for peer in peers:
            pl.semaphore_signal(barrier, inc=1, device_id=peer, device_id_type=pl.DeviceIdType.MESH)
        pl.semaphore_wait(barrier, len(peers))


def remote(source, target, sems, index, peer):
    return pltpu.make_async_remote_copy(
        src_ref=source,
        dst_ref=target,
        send_sem=sems[0].at[index],
        recv_sem=sems[1].at[index],
        device_id=peer,
        device_id_type=pl.DeviceIdType.MESH,
    )


def gather_kernel(
    size, entry_ref, few_ref, own_refs, whole_ref, gate_ref, all_ref, copies_refs, inner_ref, local, ring_sems, few_sems, rep_sems
):
    peers = Peers(size)
    half = peers.half
    rows, few_rows = inner_ref.shape[0] // 2, few_ref.shape[0] // 2
    keep = []
    for f in range(size):
        for side, target in enumerate((inner_ref, gate_ref)):
            source = ((side * size + f) * COPIES + peers.copy) * LANES
            keep.append(
                pltpu.make_async_copy(
                    entry_ref.at[:, pl.ds(pl.multiple_of(source, LANES), LANES)],
                    target.at[:, pl.ds(f * LANES, LANES)],
                    local.at[len(keep)],
                )
            )
    for copy in keep:
        copy.start()
    peers.meet()
    for copy in keep:
        copy.wait()

    sent = []

    def start(*copy):
        moving = remote(*copy)
        moving.start()
        sent.append(moving)

    for i, (own, copies) in enumerate(zip(own_refs, copies_refs)):
        start(own, copies.at[2], rep_sems, (i, 0), peers.across)
        start(own, copies.at[1], rep_sems, (i, 1), peers.core)

    def chunk(ref, c, step, n):
        return ref.at[pl.ds(c * n, n), :]

    def owner(way, step):
        return peers.at(-step if way == 0 else step)

    def come(way, step, c):
        piece = chunk(whole_ref.at[owner(way, step)], c, step, rows)
        remote(piece, piece, ring_sems, (way, step - 1, c), peers.ring[way]).wait_recv()

    def few_piece(way, step, last):
        columns = pl.ds(pl.multiple_of(owner(way, step) * LANES, LANES), LANES)
        return all_ref.at[pl.ds(way * few_rows if last else 0, few_rows * (1 if last else 2)), columns]

    def few_come(way, step):
        piece = few_piece(way, step, step == half)
        remote(piece, piece, few_sems, (way, step - 1), peers.ring[way]).wait_recv()

    for step in range(1, half + 1):
        last = step == half
        for way in range(2):
            if step > 1:
                few_come(way, step - 1)
            target = few_piece(way, step - 1, last)
            source = few_ref if step == 1 else target
            start(source, target, few_sems, (way, step - 1), peers.ring[way])
        for c in range(2):
            for way in range(2):
                if last and c != way:
                    continue
                if step > 1:
                    come(way, step - 1, c)
                target = chunk(whole_ref.at[owner(way, step - 1)], c, step, rows)
                source = chunk(inner_ref, c, step, rows) if step == 1 else target
                start(source, target, ring_sems, (way, step - 1, c), peers.ring[way])
        if step == 1:
            mine = pl.ds(pl.multiple_of(peers.member * LANES, LANES), LANES)
            keep = [
                pltpu.make_async_copy(inner_ref, whole_ref.at[peers.member], local.at[0]),
                pltpu.make_async_copy(few_ref, all_ref.at[:, mine], local.at[1]),
            ]
            for i, (own, copies) in enumerate(zip(own_refs, copies_refs)):
                keep.append(pltpu.make_async_copy(own, copies.at[0], local.at[2 + i]))
            for copy in keep:
                copy.start()
    for i, copies in enumerate(copies_refs):
        remote(copies.at[2], copies.at[2], rep_sems, (i, 0), peers.across).wait_recv()
        start(copies.at[2], copies.at[3], rep_sems, (i, 2), peers.core)
    for way in range(2):
        come(way, half - 1, 1 - way)
        come(way, half, way)
        few_come(way, half)
    for i, copies in enumerate(copies_refs):
        remote(copies.at[1], copies.at[1], rep_sems, (i, 1), peers.core).wait_recv()
        remote(copies.at[3], copies.at[3], rep_sems, (i, 2), peers.core).wait_recv()
    for moving in sent:
        moving.wait_send()
    for copy in keep:
        copy.wait()


def gather_all(size, entry, few, own):
    anywhere = pl.BlockSpec(memory_space=pl.ANY)
    count, half = len(own), size // 2
    shard = (entry.shape[0], size * LANES)

    def kernel(*refs):
        entry_ref, few_ref = refs[:2]
        own_refs = refs[2 : 2 + count]
        whole_ref, gate_ref, all_ref = refs[2 + count : 5 + count]
        copies_refs = refs[5 + count : 5 + 2 * count]
        inner_ref, local, *sems = refs[5 + 2 * count :]
        pairs = [sems[i : i + 2] for i in range(0, 6, 2)]
        gather_kernel(
            size, entry_ref, few_ref, own_refs, whole_ref, gate_ref, all_ref, copies_refs, inner_ref, local, *pairs
        )

    ring_sems = pltpu.SemaphoreType.DMA((2, half, 2))
    few_sems = pltpu.SemaphoreType.DMA((2, half))
    rep_sems = pltpu.SemaphoreType.DMA((count, 3))
    outs = [
        jax.ShapeDtypeStruct((size,) + shard, entry.dtype),
        jax.ShapeDtypeStruct(shard, entry.dtype),
        jax.ShapeDtypeStruct((few.shape[0], size * LANES), few.dtype),
    ] + [jax.ShapeDtypeStruct((COPIES,) + o.shape, o.dtype) for o in own]
    return pl.pallas_call(
        kernel,
        in_specs=[anywhere] * (2 + count),
        out_specs=[anywhere] * (3 + count),
        out_shape=outs,
        scratch_shapes=[pltpu.VMEM(shard, entry.dtype), pltpu.SemaphoreType.DMA((2 * size,))]
        + [ring_sems] * 2
        + [few_sems] * 2
        + [rep_sems] * 2,
        compiler_params=pltpu.CompilerParams(collective_id=1, has_side_effects=True),
        cost_estimate=cost(0, 4 * size * shard[0] * shard[1]),
        name="gather_all",
    )(entry, few, *own)


def scatter_kernel(
    size, grads_ref, small_ref, parts_ref, pieces_ref, small_pieces_ref, normed_ref,
    held, small_held, pair, far_out, far_in, ring_send, ring_recv, few_send, few_recv, rep_send, rep_recv, norm_send, norm_recv,
):
    peers = Peers(size)
    half = peers.half
    rows, few_rows = grads_ref.shape[1] // 2, small_ref.shape[1] // 2
    ring_sems, few_sems = (ring_send, ring_recv), (few_send, few_recv)
    rep_sems, norm_sems = (rep_send, rep_recv), (norm_send, norm_recv)
    peers.meet()
    sent = []

    def start(*copy):
        moving = remote(*copy)
        moving.start()
        sent.append(moving)

    def of_chunk(c):
        return pl.ds(c * rows, rows)

    def of_few(way):
        return pl.ds(way * few_rows, few_rows)

    def owner(way, step):
        away = half + 1 - step
        return peers.at(away if way == 0 else -away)

    def come(way, step, c):
        piece = held.at[way, step - 1, of_chunk(c), :]
        remote(piece, piece, ring_sems, (way, step - 1, c), peers.ring[way]).wait_recv()
        return piece

    def few_come(way, step):
        piece = small_held.at[way, step - 1]
        piece = piece.at[of_few(way), :] if step == 1 else piece
        remote(piece, piece, few_sems, (way, step - 1), peers.ring[way]).wait_recv()

    for way in range(2):
        start(
            grads_ref.at[owner(way, 1), of_chunk(way), :], held.at[way, 0, of_chunk(way), :],
            ring_sems, (way, 0, way), peers.ring[way],
        )
        start(
            small_ref.at[owner(way, 1), of_few(way), :], small_held.at[way, 0, of_few(way), :],
            few_sems, (way, 0), peers.ring[way],
        )
    for i in range(2):
        start(parts_ref.at[1 + 2 * i], pair.at[i], norm_sems, i, peers.core)
    for i in range(2):
        remote(pair.at[i], pair.at[i], norm_sems, i, peers.core).wait_recv()
    far_out[...] = (parts_ref[2].astype(F32) + pair[1].astype(F32)).astype(BF16)
    start(far_out, far_in, norm_sems, 2, peers.across)
    normed_ref[...] = parts_ref[0].astype(F32) + pair[0].astype(F32)

    for step in range(2, half + 1):
        for c in range(2):
            for way in range(2):
                block = owner(way, step)
                target = held.at[way, step - 1, of_chunk(c), :]
                if step == 2 and c != way:
                    source = grads_ref.at[block, of_chunk(c), :]
                else:
                    source = come(way, step - 1, c)
                    source[...] = (
                        grads_ref[block, of_chunk(c), :].astype(F32) + source[...].astype(F32)
                    ).astype(BF16)
                start(source, target, ring_sems, (way, step - 1, c), peers.ring[way])
        for way in range(2):
            block = owner(way, step)
            few_come(way, step - 1)
            source = small_held.at[way, step - 2]
            if step == 2:
                there, rest = of_few(way), of_few(1 - way)
                source[rest, :] = small_ref[block, rest, :]
            else:
                there = pl.ds(0, 2 * few_rows)
            source[there, :] = (
                small_ref[block, there, :].astype(F32) + source[there, :].astype(F32)
            ).astype(BF16)
            start(source, small_held.at[way, step - 1], few_sems, (way, step - 1), peers.ring[way])

    for c in range(2):
        at = of_chunk(c)
        for way in range(2):
            come(way, half, c)
        total = grads_ref[peers.member, at, :].astype(F32)
        for way in range(2):
            total = total + held[way, half - 1, at, :].astype(F32)
        pieces_ref[0, at, :] = total.astype(BF16)
        start(pieces_ref.at[0, at, :], pieces_ref.at[2, at, :], rep_sems, (c, 0), peers.across)
        start(pieces_ref.at[0, at, :], pieces_ref.at[1, at, :], rep_sems, (c, 1), peers.core)
    for way in range(2):
        few_come(way, half)
    total = small_ref[peers.member].astype(F32)
    for way in range(2):
        total = total + small_held[way, half - 1].astype(F32)
    small_pieces_ref[0] = total.astype(BF16)
    start(small_pieces_ref.at[0], small_pieces_ref.at[2], rep_sems, (2, 0), peers.across)
    start(small_pieces_ref.at[0], small_pieces_ref.at[1], rep_sems, (2, 1), peers.core)

    remote(far_in, far_in, norm_sems, 2, peers.across).wait_recv()
    normed_ref[...] = normed_ref[...] + far_in[...].astype(F32)

    def views(index):
        if index == 2:
            return [small_pieces_ref.at[k] for k in range(COPIES)]
        return [pieces_ref.at[k, of_chunk(index), :] for k in range(COPIES)]

    for index in range(3):
        view = views(index)
        remote(view[2], view[2], rep_sems, (index, 0), peers.across).wait_recv()
        start(view[2], view[3], rep_sems, (index, 2), peers.core)
    for index in range(3):
        view = views(index)
        remote(view[1], view[1], rep_sems, (index, 1), peers.core).wait_recv()
        remote(view[3], view[3], rep_sems, (index, 2), peers.core).wait_recv()
    for moving in sent:
        moving.wait_send()


def scatter_all(size, grads, small, parts):
    inside = pl.BlockSpec(memory_space=pltpu.VMEM)
    half = size // 2
    dma = pltpu.SemaphoreType.DMA
    return pl.pallas_call(
        functools.partial(scatter_kernel, size),
        in_specs=[inside] * 3,
        out_specs=[inside] * 3,
        out_shape=[
            jax.ShapeDtypeStruct((COPIES,) + grads.shape[1:], BF16),
            jax.ShapeDtypeStruct((COPIES,) + small.shape[1:], BF16),
            jax.ShapeDtypeStruct(parts.shape[1:], F32),
        ],
        scratch_shapes=[
            pltpu.VMEM((2, half) + grads.shape[1:], BF16),
            pltpu.VMEM((2, half) + small.shape[1:], BF16),
            pltpu.VMEM((2,) + parts.shape[1:], BF16),
            pltpu.VMEM(parts.shape[1:], BF16),
            pltpu.VMEM(parts.shape[1:], BF16),
        ]
        + [dma((2, half, 2))] * 2
        + [dma((2, half))] * 2
        + [dma((3, 3))] * 2
        + [dma((3,))] * 2,
        compiler_params=pltpu.CompilerParams(
            collective_id=2, has_side_effects=True, vmem_limit_bytes=VMEM_LIMIT
        ),
        cost_estimate=cost(0, 4 * grads.size),
        name="scatter_all",
    )(grads, small, parts)


def spread(coefs, nstate):
    terms = []
    for _ in range(3):
        term = coefs.astype(BF16)
        terms.append(term)
        coefs = coefs - term.astype(F32)
    joined = jnp.concatenate(terms, axis=1)
    return jnp.pad(joined, ((0, 0), (0, LANES - joined.shape[1])))


def spreader(nstate):
    row = lax.broadcasted_iota(jnp.int32, (LANES, 2 * nstate * LANES), 0)
    tile = lax.broadcasted_iota(jnp.int32, (LANES, 2 * nstate * LANES), 1) // LANES
    return ((row % (2 * nstate) == tile) & (row < 6 * nstate)).astype(BF16)


def folder(nstate):
    tile = lax.broadcasted_iota(jnp.int32, (2 * nstate * LANES, LANES), 0) // LANES
    column = lax.broadcasted_iota(jnp.int32, (2 * nstate * LANES, LANES), 1)
    return (tile == column).astype(BF16)


def tiled(value, width):
    return jnp.concatenate([value] * (width // LANES), axis=1)


def at_time(t):
    return pl.ds(pl.multiple_of(t * GROUP, GROUP), GROUP)


def scan_kernel(
    nstate, chunk, pre_ref, act_ref, coef_ref, spread_ref, keep_ref, rate_ref, row_ref, held_ref, *refs
):
    out_ref, step_ref, start_ref, carry_ref, wide = refs[-5:]
    width = pre_ref.shape[1]

    @pl.when(pl.program_id(0) == 0)
    def _():
        carry_ref[...] = held_ref[...]

    start_ref[0] = carry_ref[...]
    wide[...] = jnp.dot(coef_ref[...], spread_ref[...], preferred_element_type=F32)
    pre = pre_ref[...] + row_ref[0:1]
    step_ref[...] = jnp.maximum(pre, 0.0) + jnp.log1p(jnp.exp(-jnp.abs(pre)))
    for c in range(width // chunk):
        cols = slice(c * chunk, (c + 1) * chunk)

        def advance(t, states):
            at = at_time(t)
            step, act = step_ref[at, cols], act_ref[at, cols]
            drive = jnp.where(tiled(keep_ref[at, :], chunk) > 0.5, step, FAR)
            inflow = step * act
            total = row_ref[1:2, cols] * act
            now = []
            for n in range(nstate):
                write = tiled(wide[at, n * LANES : (n + 1) * LANES], chunk)
                read = tiled(wide[at, (nstate + n) * LANES : (nstate + n + 1) * LANES], chunk)
                state = jnp.exp2(drive * rate_ref[n, :, cols]) * states[n] + write * inflow
                total = total + read * state
                now.append(state)
            out_ref[at, cols] = total
            return tuple(now)

        start = tuple(carry_ref[n, :, cols] for n in range(nstate))
        states = lax.fori_loop(0, BLOCK, advance, start, unroll=4)
        for n in range(nstate):
            carry_ref[n, :, cols] = states[n]


def scan_forward(pre, act, coef, spread_by, keep, rate, rows, held, before, first, count):
    total, width = pre.shape
    nstate = rate.shape[0]
    size = BLOCK * GROUP
    tile = pl.BlockSpec((size, width), lambda t: (first + t, 0))
    thin = pl.BlockSpec((size, LANES), lambda t: (first + t, 0))
    state = pl.BlockSpec((nstate, GROUP, width), lambda t: (0, 0, 0))
    work = count * size * width * nstate
    return pl.pallas_call(
        functools.partial(scan_kernel, nstate, 256),
        grid=(count,),
        in_specs=[
            tile,
            tile,
            thin,
            pl.BlockSpec(spread_by.shape, lambda t: (0, 0)),
            thin,
            state,
            pl.BlockSpec((8, width), lambda t: (0, 0)),
            state,
        ]
        + [pl.BlockSpec(memory_space=pl.ANY)] * len(before),
        out_specs=[
            tile,
            tile,
            pl.BlockSpec((1, nstate, GROUP, width), lambda t: (first + t, 0, 0, 0)),
            state,
        ],
        out_shape=[
            jax.ShapeDtypeStruct((total, width), F32),
            jax.ShapeDtypeStruct((total, width), F32),
            jax.ShapeDtypeStruct((total // size, nstate, GROUP, width), F32),
            jax.ShapeDtypeStruct((nstate, GROUP, width), F32),
        ],
        scratch_shapes=[pltpu.VMEM((size, 2 * nstate * LANES), F32)],
        input_output_aliases={8 + i: i for i in range(len(before))},
        compiler_params=params(),
        cost_estimate=cost(16 * work, 16 * count * size * width),
        name="scan_forward",
    )(pre, act, coef, spread_by, keep, rate, rows, held, *before)


class Guests:
    def __init__(self, size, parts, totals, held, sems):
        self.peers = Peers(size)
        self.parts, self.totals, self.held, self.sems = parts, totals, held, sems

    def rows(self, which, c):
        half = self.parts[which].shape[1] // 2
        return pl.ds(c * half, half)

    def copy(self, which, way, step, c, source=None):
        target = self.held[which].at[way, step - 1, self.rows(which, c), :]
        index = (which, way, step - 1, c)
        source = target if source is None else source
        return remote(source, target, self.sems, index, self.peers.ring[way])

    def chunks(self, way, step):
        return (way,) if step == 1 else (0, 1)

    def own(self, which, way, step, c):
        away = self.peers.half + 1 - step
        block = self.peers.at(away if way == 0 else -away)
        return self.parts[which].at[block, self.rows(which, c), :]

    def source(self, which, way, step, c):
        own = self.own(which, way, step, c)
        if step == 1 or c not in self.chunks(way, step - 1):
            return own
        self.copy(which, way, step - 1, c).wait_recv()
        there = self.held[which].at[way, step - 2, self.rows(which, c), :]
        there[...] = (own[...].astype(F32) + there[...].astype(F32)).astype(BF16)
        return there

    def tick(self, number):
        which, step = number % 2, number // 2 + 1
        for c in range(2):
            for way in range(2):
                if c in self.chunks(way, step):
                    self.copy(which, way, step, c, self.source(which, way, step, c)).start()

    def finish(self):
        last = self.peers.half
        for which in range(2):
            for c in range(2):
                total = self.own(which, 0, last + 1, c)[...].astype(F32)
                for way in range(2):
                    self.copy(which, way, last, c).wait_recv()
                    there = self.held[which].at[way, last - 1, self.rows(which, c), :]
                    total = total + there[...].astype(F32)
                self.totals[which][self.rows(which, c), :] = total.astype(BF16)
        for which in range(2):
            for step in range(1, last + 1):
                for way in range(2):
                    for c in self.chunks(way, step):
                        self.copy(which, way, step, c).wait_send()


def scan_back_kernel(
    nstate, chunk, rings, pre_ref, step_ref, act_ref, grad_ref, coef_ref, spread_ref, fold_ref, keep_ref, rate_ref,
    row_ref, start_ref, *refs,
):
    wide, states_all, decays, parts, sizes = refs[-5:]
    width = pre_ref.shape[1]
    step_now = pl.program_id(0)
    if rings:
        first_ref, second_ref = refs[:2]
        pre_grad_ref, direct_ref, coef_grad_ref, carry_ref, sums_ref = refs[2:7]
        guest = Guests(rings, (first_ref, second_ref), refs[7:9], refs[9:11], refs[11:13])
        for tick in range(2 * guest.peers.half):

            @pl.when(step_now == tick)
            def _(tick=tick):
                if tick == 0:
                    guest.peers.meet()
                guest.tick(tick)

    else:
        pre_grad_ref, direct_ref, coef_grad_ref, carry_ref, sums_ref = refs[-10:-5]

    @pl.when(step_now == 0)
    def _():
        carry_ref[...] = jnp.zeros_like(carry_ref)
        sums_ref[...] = jnp.zeros_like(sums_ref)

    wide[...] = jnp.dot(coef_ref[...], spread_ref[...], preferred_element_type=F32)

    def fold(value):
        total = value[:, :LANES]
        for k in range(1, chunk // LANES):
            total = total + value[:, k * LANES : (k + 1) * LANES]
        return total

    for c in range(width // chunk):
        cols = slice(c * chunk, (c + 1) * chunk)

        def advance(t, states):
            at = at_time(t)
            step = step_ref[at, cols]
            drive = jnp.where(tiled(keep_ref[at, :], chunk) > 0.5, step, FAR)
            inflow = step * act_ref[at, cols]
            now = []
            for n in range(nstate):
                write = tiled(wide[at, n * LANES : (n + 1) * LANES], chunk)
                decay = jnp.exp2(drive * rate_ref[n, :, cols])
                decays[t, n] = decay
                states_all[t, n] = states[n]
                now.append(decay * states[n] + write * inflow)
            return tuple(now)

        start = tuple(start_ref[0, n, :, cols] for n in range(nstate))
        states = lax.fori_loop(0, BLOCK, advance, start, unroll=2)
        for n in range(nstate):
            states_all[BLOCK, n] = states[n]

        def retreat(i, carry):
            t = BLOCK - 1 - i
            at = at_time(t)
            step, act, grad = step_ref[at, cols], act_ref[at, cols], grad_ref[at, cols]
            inflow = step * act
            size = jnp.zeros_like(step)
            direct = jnp.zeros_like(step)
            now = []
            for n in range(nstate):
                tile_w = slice(n * LANES, (n + 1) * LANES)
                tile_r = slice((nstate + n) * LANES, (nstate + n + 1) * LANES)
                state_grad = tiled(wide[at, tile_r], chunk) * grad + carry[n]
                passed = decays[t, n] * state_grad
                through = passed * states_all[t, n]
                size = size + rate_ref[n, :, cols] * through
                direct = direct + state_grad * tiled(wide[at, tile_w], chunk)
                sums_ref[n, :, cols] += step * through
                write_part = fold(state_grad * inflow)
                read_part = fold(grad * states_all[t + 1, n])
                if c == 0:
                    parts[at, tile_w] = write_part
                    parts[at, tile_r] = read_part
                else:
                    parts[at, tile_w] += write_part
                    parts[at, tile_r] += read_part
                now.append(passed)
            sizes[at, cols] = LN2 * size + act * direct
            direct_ref[at, cols] = step * direct + row_ref[1:2, cols] * grad
            sums_ref[nstate, :, cols] += grad * act
            return tuple(now)

        start = tuple(carry_ref[n, :, cols] for n in range(nstate))
        carry = lax.fori_loop(0, BLOCK, retreat, start, unroll=2)
        for n in range(nstate):
            carry_ref[n, :, cols] = carry[n]

    pre_grad = sizes[...] * sigmoid(pre_ref[...] + row_ref[0:1])
    pre_grad_ref[...] = pre_grad.astype(BF16)
    total = pre_grad[:GROUP]
    for t in range(1, BLOCK):
        total = total + pre_grad[t * GROUP : (t + 1) * GROUP]
    sums_ref[nstate + 1] += total
    high = parts[...].astype(BF16)
    low = (parts[...] - high.astype(F32)).astype(BF16)
    coef_grad_ref[...] = jnp.dot(high, fold_ref[...], preferred_element_type=F32) + jnp.dot(
        low, fold_ref[...], preferred_element_type=F32
    )
    if rings:

        @pl.when(step_now == pl.num_programs(0) - 1)
        def _():
            guest.finish()


def scan_backward(
    pre, step, act, grad, coef, spread_by, fold_by, keep, rate, rows, starts, rings, wgrads
):
    total, width = pre.shape
    nstate = rate.shape[0]
    size = BLOCK * GROUP
    chunk = 256
    count = total // size
    tile = pl.BlockSpec((size, width), lambda t: (count - 1 - t, 0))
    thin = pl.BlockSpec((size, LANES), lambda t: (count - 1 - t, 0))
    state = pl.BlockSpec((nstate, GROUP, width), lambda t: (0, 0, 0))
    tally = pl.BlockSpec((nstate + 2, GROUP, width), lambda t: (0, 0, 0))
    work = count * size * width * nstate
    inside = pl.BlockSpec(memory_space=pltpu.VMEM)
    half = rings // 2
    guests = [jax.ShapeDtypeStruct(w.shape[1:], BF16) for w in wgrads]
    sems = [pltpu.SemaphoreType.DMA((2, 2, half, 2))] * 2 if rings else []
    return pl.pallas_call(
        functools.partial(scan_back_kernel, nstate, chunk, rings),
        grid=(count,),
        in_specs=[
            tile,
            tile,
            tile,
            tile,
            thin,
            pl.BlockSpec(spread_by.shape, lambda t: (0, 0)),
            pl.BlockSpec(fold_by.shape, lambda t: (0, 0)),
            thin,
            state,
            pl.BlockSpec((8, width), lambda t: (0, 0)),
            pl.BlockSpec((1, nstate, GROUP, width), lambda t: (count - 1 - t, 0, 0, 0)),
        ]
        + [inside] * len(wgrads),
        out_specs=[tile, tile, thin, state, tally] + [inside] * len(wgrads),
        out_shape=[
            jax.ShapeDtypeStruct((total, width), BF16),
            jax.ShapeDtypeStruct((total, width), F32),
            jax.ShapeDtypeStruct((total, LANES), F32),
            jax.ShapeDtypeStruct((nstate, GROUP, width), F32),
            jax.ShapeDtypeStruct((nstate + 2, GROUP, width), F32),
        ]
        + guests,
        scratch_shapes=[pltpu.VMEM((2, half) + w.shape[1:], BF16) for w in wgrads]
        + sems
        + [
            pltpu.VMEM((size, 2 * nstate * LANES), F32),
            pltpu.VMEM((BLOCK + 1, nstate, GROUP, chunk), F32),
            pltpu.VMEM((BLOCK, nstate, GROUP, chunk), F32),
            pltpu.VMEM((size, 2 * nstate * LANES), F32),
            pltpu.VMEM((size, width), F32),
        ],
        compiler_params=pltpu.CompilerParams(
            collective_id=3, has_side_effects=True, vmem_limit_bytes=VMEM_LIMIT
        )
        if rings
        else params(),
        cost_estimate=cost(40 * work, 24 * count * size * width),
        name="scan_backward",
    )(pre, step, act, grad, coef, spread_by, fold_by, keep, rate, rows, starts, *wgrads)


def spread_columns_kernel(copy_ref, *refs):
    pieces, weight_ref, out_ref, gain_ref = refs[:4], refs[4], refs[-2], refs[-1]
    part = pieces[0].shape[1]

    @pl.when(pl.program_id(0) == 0)
    def _():
        gain_ref[...] = jnp.zeros_like(gain_ref)

    total = gain_ref[...]
    for k, piece in enumerate(pieces):
        at = pl.ds(pl.multiple_of((copy_ref[0] ^ k) * part, part), part)
        value = piece[...].astype(F32)
        out_ref[:, at] = value
        total = total + value * weight_ref[:, at].astype(F32)
    gain_ref[...] = total


def spread_columns(copy, pieces, weight, side, before=None):
    rows, width = pieces[0].shape
    part = LANES
    shares = width // part
    block = pl.BlockSpec((rows, COPIES * part), lambda f, copy: (0, side * shares + f))
    piece = pl.BlockSpec((rows, part), lambda f, copy: (0, f))
    extra = [] if before is None else [before]
    return pl.pallas_call(
        spread_columns_kernel,
        grid_spec=pltpu.PrefetchScalarGridSpec(
            num_scalar_prefetch=1,
            grid=(shares,),
            in_specs=[piece] * 4 + [block] + [pl.BlockSpec(memory_space=pl.ANY)] * len(extra),
            out_specs=[block, pl.BlockSpec((rows, part), lambda f, copy: (0, 0))],
        ),
        out_shape=[
            jax.ShapeDtypeStruct(weight.shape, F32),
            jax.ShapeDtypeStruct((rows, part), F32),
        ],
        input_output_aliases={6: 0} if extra else {},
        compiler_params=params(),
        cost_estimate=cost(4 * rows * width, 20 * rows * width),
        name="spread_columns",
    )(copy, *pieces, weight, *extra)


def spread_rows_kernel(copy_ref, *refs):
    pieces, out_ref = refs[:4], refs[4]
    part = pieces[0].shape[0]
    for k, piece in enumerate(pieces):
        at = pl.ds(pl.multiple_of((copy_ref[0] ^ k) * part, part), part)
        out_ref[at, :] = piece[...].astype(F32)


def spread_rows(copy, pieces):
    part, columns = pieces[0].shape
    tile = 512
    return pl.pallas_call(
        spread_rows_kernel,
        grid_spec=pltpu.PrefetchScalarGridSpec(
            num_scalar_prefetch=1,
            grid=(columns // tile,),
            in_specs=[pl.BlockSpec((part, tile), lambda c, copy: (0, c))] * 4,
            out_specs=pl.BlockSpec((COPIES * part, tile), lambda c, copy: (0, c)),
        ),
        out_shape=jax.ShapeDtypeStruct((COPIES * part, columns), F32),
        compiler_params=params(),
        cost_estimate=cost(4 * part * columns, 24 * part * columns),
        name="spread_rows",
    )(copy, *pieces)


def on_device(
    tokens, segment_ids, out_grad, norm_gain, in_proj, conv_weight, conv_bias, x_proj,
    step_proj, step_bias, decay_log, skip_gain, out_proj, *, fsdp,
):
    ring = Ring(fsdp)
    copy = lax.axis_index("rep")
    batches, length, model = tokens.shape
    total = COPIES * batches * length
    slab = in_proj.shape[0]
    share = out_proj.shape[0]
    part = share // COPIES
    width = fsdp * part
    rank, nstate = step_proj.shape[1], decay_log.shape[1]
    taps_n = conv_weight.shape[1]
    gains_n = slab // part

    def mine(value):
        return lax.dynamic_slice_in_dim(value, copy * part, part, 0)

    copy_index = copy.astype(jnp.int32).reshape(1)
    aligned = part % LANES == 0
    if not aligned:
        entry = lax.dynamic_index_in_dim(
            in_proj.reshape(slab, 2, fsdp, COPIES, part), copy, 3, keepdims=False
        )
        inner_shard, gate_shard = (entry[:, i].reshape(slab, width) for i in range(2))
    few = jnp.concatenate(
        [
            mine(x_proj).T,
            mine(step_proj).T,
            mine(conv_weight).T,
            mine(conv_bias)[None],
            mine(step_bias)[None],
            mine(decay_log).T,
            mine(skip_gain)[None],
            norm_gain.reshape(gains_n, part),
        ],
        axis=0,
    )
    few = jnp.pad(few, ((0, -few.shape[0] % 16), (0, 0)))
    small_ring = ring.half == 4
    own = [tokens, out_grad, segment_ids[:, 0, :]]
    if small_ring and aligned:
        inner_in, gate_shard, few_all, *copies = gather_all(fsdp, in_proj, few, own)
        few_all = few_all.astype(F32)
    else:
        gathers = [Gather(ring, inner_shard), Gather(ring, few)]
        for gather in gathers:
            gather.rest()
        inner_in, few_all = (gather.whole for gather in gathers)
        few_all = jnp.moveaxis(few_all, 0, 1).reshape(-1, width).astype(F32)
        copies = [jnp.stack(rep_gather(value)) for value in own]
    inner_in, out_shard = lax.optimization_barrier((inner_in, mine(out_proj)))
    gate_gather = Gather(ring, gate_shard)
    out_gather = Gather(ring, out_shard)
    inner_in = inner_in.reshape(model, width)
    values, cotangent, segments = (c.reshape((GROUP,) + c.shape[2:]) for c in copies)

    sizes = [rank + 2 * nstate, rank, taps_n, 1, 1, nstate, 1, gains_n]
    pieces, start = [], 0
    for size in sizes:
        pieces.append(few_all[start : start + size])
        start += size
    select, stride, taps, shift_bias, size_bias, decay, skip, gain = pieces
    select, stride = select.astype(BF16), stride.astype(BF16)
    gain = jnp.moveaxis(gain.reshape(gains_n, fsdp, part), 0, 1).reshape(model)

    def masks_of(segments):
        masks = []
        for shift in range(1, taps_n):
            earlier = jnp.pad(segments, ((0, 0), (shift, 0)), constant_values=-1)[:, :length]
            masks.append((earlier == segments).astype(F32).T.reshape(total, 1))
        return jnp.broadcast_to(jnp.stack(masks), (taps_n - 1, total, LANES))

    def small_terms():
        tap_rows = jnp.concatenate(
            [taps, shift_bias, jnp.zeros((7 - taps_n, width), F32)]
        )
        side_rows = jnp.concatenate(
            [size_bias, skip, jnp.zeros((6, width), F32)]
        )
        decay_rate = -jnp.exp(decay)
        rate = jnp.broadcast_to((decay_rate * LOG2E)[:, None, :], (nstate, GROUP, width))
        return tap_rows, side_rows, decay_rate, rate, masks_of(segments), spreader(nstate), folder(nstate)

    tap_rows, side_rows, decay_rate, rate, masks, spread_by, fold_by = small_terms()
    normed = interleave(values, gain)
    keep = masks[0]

    state0 = jnp.zeros((nstate, GROUP, width), F32)
    blocks = length // BLOCK
    store = {}

    def g1():
        inner = dot(normed, inner_in, 1, 0)
        return (inner,) + tuple(conv_forward(inner, masks, tap_rows))

    def g2():
        part_sums = dot(store["act_low"], select, 1, 1)
        return sum_near(by_copy(part_sums))

    def g3():
        projected = to_time(sum_far(store["half_sums"]).reshape(total, -1))
        store["step_low"] = projected[:, :rank].astype(BF16)
        store["coef"] = spread(projected[:, rank:], nstate)
        store["pre"] = dot(store["step_low"], stride, 1, 0)
        return store["step_low"], store["coef"], store["pre"], forward_part(0, (), state0)

    def forward_part(first, before, held):
        return tuple(
            scan_forward(
                store["pre"], store["act"], store["coef"], spread_by, keep, rate, side_rows,
                held, before, first, blocks // 2,
            )
        )

    def g4():
        out = store["scan"]
        return forward_part(blocks // 2, out[:3], out[3])

    movers = [gate_gather] if small_ring else []
    ((store["inner"], store["act"], store["act_low"]),) = slot(1, movers, g1)
    (store["half_sums"],) = slot(2, movers, g2)
    ((store["step_low"], store["coef"], store["pre"], store["scan"]),) = slot(3, movers, g3)
    (store["scan"],) = slot(4, movers, g4)
    if not small_ring:
        gate_gather.rest()
    readout, step, starts, _ = store["scan"]
    gate_in = gate_gather.whole.reshape(model, width)

    def o1():
        return dot(normed, gate_in, 1, 0)

    def o2():
        return gate_forward(readout, store["gate"])

    def o3():
        return dot(gated, cotangent, 0, 0).astype(BF16).reshape(fsdp, part, model)

    movers = [out_gather] if small_ring else []
    (store["gate"],) = slot(1, movers, o1)
    (gated, gated_natural), cotangent = slot(2, movers, o2, lambda: interleave(cotangent))
    (out_wgrad,) = slot(3, movers, o3)
    slot(4, movers)
    if not small_ring:
        out_gather.rest()
    out_w = out_gather.whole.reshape(width, model)
    gate, inner, act, act_low = (store[k] for k in ("gate", "inner", "act", "act_low"))
    pre, coef, step_low = store["pre"], store["coef"], store["step_low"]

    fused = small_ring and aligned
    def r1():
        return gate_backward(dot(cotangent, out_w, 1, 1), readout, gate)

    read_grad, gate_grad, gate_grad_natural = r1()

    gate_wgrad = dot(normed, gate_grad, 0, 0).astype(BF16).reshape(fsdp, slab, width)
    wgrads = [out_wgrad, gate_wgrad] if fused else []
    pre_low, direct, coef_part, _, sums, *totals = scan_backward(
        pre, step, act, read_grad, coef, spread_by, fold_by, keep, rate, side_rows, starts,
        fsdp if fused else 0, wgrads,
    )
    if not fused:
        scatters = [Scatter(ring, out_wgrad), Scatter(ring, gate_wgrad)]
        for scatter in scatters:
            scatter.rest()
        totals = [scatter.total.astype(BF16) for scatter in scatters]
    low_part = dot(pre_low, stride, 1, 1)
    proj_part = jnp.concatenate([low_part, coef_part[:, : 2 * nstate]], axis=1)
    gated_natural, gate_grad_natural = after(pre_low, gated_natural, gate_grad_natural)

    def norm_gate_part():
        return dot(gate_grad_natural, gate_in, 1, 1)

    def out_part():
        return by_copy(dot(gated_natural, out_w, 1, 0).astype(BF16))

    def proj_sums():
        return sum_near(by_copy(to_sequence(proj_part)))

    half_sums, out_parts, norm_gate, out_pieces = slot(
        3, [], proj_sums, out_part, norm_gate_part, lambda: rep_gather(totals[0])
    )

    def conv_part():
        proj_low = sum_far(half_sums).reshape(total, -1).astype(BF16)
        act_grad = direct + dot(to_time(proj_low), select, 1, 0)
        inner_grad, inner_grad_natural, conv_sums = conv_backward(inner, act_grad, masks, tap_rows)
        inner_wgrad = dot(normed, inner_grad, 0, 0).astype(BF16).reshape(fsdp, slab, width)
        small = jnp.concatenate(
            [
                dot(proj_low, act_low, 0, 0),
                dot(step_low, pre_low, 0, 0),
                conv_sums[: taps_n + 1],
                jnp.sum(sums[nstate + 1 :], axis=1),
                decay_rate * jnp.sum(sums[:nstate], axis=1),
                jnp.sum(sums[nstate : nstate + 1], axis=1),
            ],
            axis=0,
        )
        small = jnp.pad(small, ((0, -small.shape[0] % 16), (0, 0))).astype(BF16)
        small = jnp.moveaxis(small.reshape(-1, fsdp, part), 1, 0)
        return inner_grad_natural, inner_wgrad, small

    (inner_grad_natural, inner_wgrad, small), (out_near, out_far) = slot(
        4, [], conv_part, lambda: rep_scatter_near(out_parts)
    )

    grads = dot(inner_grad_natural, inner_in, 1, 1) + norm_gate
    norm_parts = by_copy(grads.astype(BF16))

    def finish_out():
        summed = rep_scatter_far(out_near, out_far)
        return (tokens.astype(F32) + summed.reshape(tokens.shape)).astype(BF16)

    gate_pieces = rep_gather(totals[1])

    def place_gate():
        if not aligned:
            return gate_pieces
        return spread_columns(copy_index, gate_pieces, in_proj, 1)

    def place_out():
        if aligned:
            return spread_rows(copy_index, out_pieces)
        return jnp.stack(out_pieces)[jnp.arange(COPIES) ^ copy].reshape(share, model).astype(F32)

    gate_placed, out_all, block_out = place_gate(), place_out(), finish_out()
    if small_ring and aligned:
        inner_pieces, small_pieces, normed_sum = scatter_all(fsdp, inner_wgrad, small, norm_parts)
        inner_pieces = [inner_pieces[k] for k in range(COPIES)]
        small_pieces = [small_pieces[k] for k in range(COPIES)]
    else:
        near, far = rep_scatter_near(norm_parts)
        normed_sum = rep_scatter_far(near, far)
        scatters = [Scatter(ring, inner_wgrad), Scatter(ring, small)]
        for scatter in scatters:
            scatter.rest()
        inner_pieces, small_pieces = (rep_gather(s.total.astype(BF16)) for s in scatters)

    def finish_tokens():
        normed_grad = normed_sum.reshape(tokens.shape)
        own = tokens.astype(F32)
        own_scale = lax.rsqrt(jnp.mean(own * own, axis=-1, keepdims=True) + EPS)
        scaled = normed_grad * gain
        lean = jnp.mean(scaled * own, axis=-1, keepdims=True)
        return (
            out_grad.astype(F32) + own_scale * scaled - own * (own_scale**3) * lean
        ).astype(BF16)

    input_grad = finish_tokens()

    order = jnp.arange(COPIES) ^ copy
    if aligned:
        entry_all, gain_inner = spread_columns(
            copy_index, inner_pieces, in_proj, 0, gate_placed[0]
        )
        gain_sum = jnp.sum(gain_inner + gate_placed[1], axis=1)
    else:
        halves = jnp.stack([jnp.stack(inner_pieces), jnp.stack(gate_placed)])[:, order]
        halves = halves.reshape(2, COPIES, slab, fsdp, part).astype(F32)
        entry_all = jnp.transpose(halves, (2, 0, 3, 1, 4)).reshape(slab, -1)
        gain_sum = jnp.sum(entry_all * in_proj.astype(F32), axis=1)
    gain_grad = gain_sum / norm_gain.astype(F32)
    small_all = jnp.stack(small_pieces)[order].astype(F32)
    small_all = jnp.moveaxis(small_all, 0, 1).reshape(-1, share)
    out, start = [], 0
    for size in sizes[:-1]:
        out.append(small_all[start : start + size])
        start += size
    select_g, stride_g, taps_g, shift_g, size_g, decay_g, skip_g = out
    return (
        block_out,
        input_grad,
        gain_grad,
        entry_all,
        taps_g.T,
        shift_g[0],
        select_g.T,
        stride_g.T,
        size_g[0],
        decay_g.T,
        skip_g[0],
        out_all,
    )


def solution(mesh):
    tokens = P(None, ("fsdp", "rep"), None)
    rows, row = P("fsdp", None), P("fsdp")
    return jax.shard_map(
        functools.partial(on_device, fsdp=mesh.shape["fsdp"]),
        mesh=mesh,
        in_specs=(tokens, tokens, tokens, row, rows, rows, row, rows, rows, row, rows, row, rows),
        out_specs=(tokens, tokens, row, rows, rows, row, rows, rows, row, rows, row, rows),
        check_vma=False,
    )
```

profile of v0, /device:TPU:0, one launch (start us, length us, event | category | flops | bytes accessed | tf_op | source)
XLA Modules:
  0.0 614.1 jit_solution(17305099158694143349)
XLA Ops:
  7.0 84.9 %gather_all.1 = (bf16[8,256,1024]{2,1,0:T(8,128)(2,1)}, bf16[256,1024]{1,0:T(8,128)(2,1)}, bf16[320,1024]{1,0:T(8,128)(2,1)}, bf16[4,2,128,2048]{3,2,1,0:T(8,128...) custom-call(bf16[256,8192]{1,0:T(8,128)(2,1)} %refs_4_.3, bf16[320,128]{1,0:T(8,128)(2,1)} %pad.26.refs_1_, ...), custom_call_target="tpu_custom_call" | custom-call | bytes 8388608 | tf_op jit(solution)/shard_map/gather_all/pallas_call | solution.py:539
  91.8 3.1 collective-permute-start
  95.0 2.1 collective-permute-start.11
  102.0 8.5 %interleave.2 = bf16[1024,2048]{1,0:T(8,128)(2,1)} custom-call(bf16[8,128,2048]{2,1,0:T(8,128)(2,1)} %bitcast.214, f32[1,2048]{1,0:T(1,128)} %bitcast.224), custom_call_target="tpu_custom_call" | custom-call | flops 16777216 | bytes 8388608 | tf_op jit(solution)/shard_map/interleave/pallas_call | solution.py:371
  110.6 8.3 %fusion.49.inner_ref = f32[1024,1024]{1,0:T(8,128)} fusion(bf16[1024,2048]{1,0:T(8,128)(2,1)} %interleave.2, bf16[2048,1024]{1,0:T(8,128)(2,1)S(1)} %bitcast.234), kind=kOutput, calls=%fused_computation.152 | convolution fusion | flops 4294967296 | bytes 12582912 | tf_op jit(solution)/shard_map/dot_general | solution.py:24
  119.7 4.7 fusion.8.fold_ref
  151.3 7.8 %interleave.3 = bf16[1024,2048]{1,0:T(8,128)(2,1)} custom-call(bf16[8,128,2048]{2,1,0:T(8,128)(2,1)} %bitcast.215), custom_call_target="tpu_custom_call" | custom-call | flops 16777216 | bytes 8388608 | tf_op jit(solution)/shard_map/interleave/pallas_call | solution.py:371
  159.1 1.7 broadcast_in_dim.94.masks_ref
  160.8 9.8 %conv_forward.1 = (f32[1024,1024]{1,0:T(8,128)}, bf16[1024,1024]{1,0:T(8,128)(2,1)}) custom-call(f32[1024,1024]{1,0:T(8,128)} %fusion.49.inner_ref, f32[3,1024,128]{2,1,0:T(8,128)} %broadcast_in_dim.94.masks_ref, f32[8,1024]{1,0:T(8,128)} %concatenate.20.taps_ref), custom_call_target="tpu_custom_call" | custom-call | flops 31457280 | bytes 10485760 | tf_op jit(solution)/shard_map/conv_forward/pallas_call | solution.py:246
  171.5 2.4 fusion.17
  174.9 1.9 collective-permute-start.2
  177.1 2.0 collective-permute-start.5
  179.9 1.9 bitcast_dynamic-update-slice_fusion.11
  181.8 5.2 collective-permute-done.5
  187.0 2.6 collective-permute-done.2
  189.6 1.7 collective-permute-done.3
  191.3 1.7 collective-permute-start.6
  193.5 1.9 bitcast_dynamic-update-slice_fusion.10
  195.4 1.9 bitcast_dynamic-update-slice_fusion.9
  199.8 2.7 fusion.23.pre_ref
  205.2 15.6 %scan_forward.2 = (f32[1024,1024]{1,0:T(8,128)}, f32[1024,1024]{1,0:T(8,128)}, f32[8,16,8,1024]{3,2,1,0:T(8,128)}, f32[16,8,1024]{2,1,0:T(8,128)}) custom-call(f32[1024,1024]{1,0:T(8,128)} %fusion.23.pre_ref, f32[1024,1024]{1,0:T(8,128)} %get-tuple-element.114.act_ref, bf16[1024,128]{1,0:T(8,128)(2,1)} %fusion.20.coef_ref, ...), custom_call_target="tpu_custom_call" | custom-call | flops 134217728 | bytes 8388608 | tf_op jit(solution)/shard_map/scan_forward/pallas_call | solution.py:783
  221.8 1.6 collective-permute-start.9
  224.9 1.9 bitcast_dynamic-update-slice_fusion.8
  226.8 15.8 %scan_forward.3 = (f32[1024,1024]{1,0:T(8,128)}, f32[1024,1024]{1,0:T(8,128)}, f32[8,16,8,1024]{3,2,1,0:T(8,128)}, f32[16,8,1024]{2,1,0:T(8,128)}) custom-call(f32[1024,1024]{1,0:T(8,128)} %fusion.23.pre_ref, f32[1024,1024]{1,0:T(8,128)} %get-tuple-element.114.act_ref, ...), custom_call_target="tpu_custom_call", output_to_operand_aliasing={{0}: (8, {}), {1}: (9, {}), {2}: (10, {})} | custom-call | flops 134217728 | bytes 8388608 | tf_op jit(solution)/shard_map/scan_forward/pallas_call | solution.py:783
  242.6 1.9 bitcast_dynamic-update-slice_fusion.7
  245.9 8.3 %fusion.50.gate_ref = f32[1024,1024]{1,0:T(8,128)} fusion(bf16[1024,2048]{1,0:T(8,128)(2,1)S(1)} %copy-done.8, bf16[2048,1024]{1,0:T(8,128)(2,1)} %bitcast.51), kind=kOutput, calls=%fused_computation.153 | convolution fusion | flops 4294967296 | bytes 12582912 | tf_op jit(solution)/shard_map/dot_general | solution.py:24
  254.2 1.6 collective-permute-start.13
  256.2 1.9 bitcast_dynamic-update-slice_fusion.5
  258.1 8.2 %gate_forward.1 = (bf16[1024,1024]{1,0:T(8,128)(2,1)}, bf16[1024,1024]{1,0:T(8,128)(2,1)}) custom-call(f32[1024,1024]{1,0:T(8,128)} %get-tuple-element.136.readout_ref, f32[1024,1024]{1,0:T(8,128)} %fusion.50.gate_ref), custom_call_target="tpu_custom_call" | custom-call | flops 20971520 | bytes 12582912 | tf_op jit(solution)/shard_map/gate_forward/pallas_call | solution.py:314
  266.3 1.9 bitcast_dynamic-update-slice_fusion.4
  268.9 1.5 collective-permute-start.15
  270.9 9.4 %convolution_convert_fusion.3 = bf16[1024,2048]{1,0:T(8,128)(2,1)} fusion(bf16[1024,1024]{1,0:T(8,128)(2,1)} %get-tuple-element.144, bf16[1024,2048]{1,0:T(8,128)(2,1)} %interleave.3), kind=kOutput, calls=%fused_computation.5 | convolution fusion | flops 4297064448 | bytes 10485760 | tf_op jit(solution)/shard_map/dot_general | solution.py:24
  283.1 1.5 collective-permute-start.17
  286.4 3.0 collective-permute-done.17
  289.4 2.0 collective-permute-done.18
  292.9 8.2 %fusion.51.grad_ref = f32[1024,1024]{1,0:T(8,128)} fusion(bf16[1024,2048]{1,0:T(8,128)(2,1)S(1)} %copy-done.11, bf16[1024,2048]{1,0:T(8,128)(2,1)} %bitcast.63), kind=kOutput, calls=%fused_computation.154 | convolution fusion | flops 4294967296 | bytes 12582912 | tf_op jit(solution)/shard_map/dot_general | solution.py:24
  301.1 11.0 %gate_backward.1 = (f32[1024,1024]{1,0:T(8,128)}, bf16[1024,1024]{1,0:T(8,128)(2,1)}, bf16[1024,1024]{1,0:T(8,128)(2,1)}) custom-call(f32[1024,1024]{1,0:T(8,128)} %fusion.51.grad_ref, f32[1024,1024]{1,0:T(8,128)} %get-tuple-element.136.readout_ref, f32[1024,1024]{1,0:T(8,128)} %fusion.50.gate_ref), custom_call_target="tpu_custom_call" | custom-call | flops 20971520 | bytes 20971520 | tf_op jit(solution)/shard_map/gate_backward/pallas_call | solution.py:339
  312.1 7.8 %convolution_convert_fusion.2 = bf16[2048,1024]{1,0:T(8,128)(2,1)} fusion(bf16[1024,2048]{1,0:T(8,128)(2,1)S(1)} %copy-done.8, bf16[1024,1024]{1,0:T(8,128)(2,1)} %get-tuple-element.152), kind=kOutput, calls=%fused_computation.4 | convolution fusion | flops 4297064448 | bytes 10485760 | tf_op jit(solution)/shard_map/dot_general | solution.py:24
  319.9 94.0 %scan_backward.1 = (bf16[1024,1024]{1,0:T(8,128)(2,1)}, f32[1024,1024]{1,0:T(8,128)}, f32[1024,128]{1,0:T(8,128)}, f32[16,8,1024]{2,1,0:T(8,128)}, f32[18,8,1024...) custom-call(f32[1024,1024]{1,0:T(8,128)} %fusion.23.pre_ref, ...), custom_call_target="tpu_custom_call" | custom-call | flops 671088640 | bytes 25165824 | tf_op jit(solution)/shard_map/scan_backward/pallas_call | solution.py:1001
  413.9 1.6 collective-permute-start.22
  417.4 2.4 fusion.21
  422.0 7.5 %convolution_convert_fusion.1 = bf16[1024,2048]{1,0:T(8,128)(2,1)S(1)} fusion(bf16[1024,1024]{1,0:T(8,128)(2,1)} %get-tuple-element.158, bf16[1024,2048]{1,0:T(8,128)(2,1)} %bitcast.63), kind=kOutput, calls=%fused_computation.3 | convolution fusion | flops 4297064448 | bytes 10485760 | tf_op jit(solution)/shard_map/dot_general | solution.py:24
  429.5 10.5 %fusion.52 = f32[1024,2048]{1,0:T(8,128)} fusion(bf16[1024,1024]{1,0:T(8,128)(2,1)S(1)} %copy-done.26, bf16[2048,1024]{1,0:T(8,128)(2,1)} %bitcast.51), kind=kOutput, calls=%fused_computation.155 | convolution fusion | flops 4294967296 | bytes 14680064 | tf_op jit(solution)/shard_map/dot_general | solution.py:24
  441.2 1.6 collective-permute-start.20
  443.9 7.4 %collective-permute-done.20 = f32[2,256,160]{1,2,0:T(8,128)S(1)} collective-permute-done((f32[2,256,160]{1,2,0:T(8,128)S(1)}, f32[2,256,160]{1,2,0:T(8,128)S(1)}, u32[]{:S(2)}, u32[]{:S(2)}) %collective-permute-start.20) | collective-permute-done | bytes 327712 | tf_op jit(solution)/shard_map/ppermute | solution.py:164
  451.7 1.5 pad_maximum_fusion
  453.7 4.2 spread_rows.1
  458.7 7.1 %spread_columns.2 = (f32[256,8192]{1,0:T(8,128)}, f32[256,128]{1,0:T(8,128)}) custom-call(s32[1]{0:T(128)} %bitcast.80.copy_ref, bf16[256,1024]{1,0:T(8,128)(2,1)} %get-tuple-element.176.refs_0_, bf16[256,1024]{1,0:T(8,128)(2,1)} %collective-permute-done.27.refs_1_, bf16[256,1024]{1,0:T(8,128)(2,1)} %collective-permute-done.28.refs_2_, ...), custom_call_target="tpu_custom_call" | custom-call | flops 1048576 | bytes 5242880 | tf_op jit(solution)/shard_map/spread_columns/pallas_call | solution.py:1070
  469.0 3.0 add.362.grad_ref
  471.9 14.2 %conv_backward.1 = (bf16[1024,1024]{1,0:T(8,128)(2,1)}, bf16[1024,1024]{1,0:T(8,128)(2,1)}, f32[8,1024]{1,0:T(8,128)}) custom-call(f32[1024,1024]{1,0:T(8,128)} %fusion.49.inner_ref, f32[1024,1024]{1,0:T(8,128)} %add.362.grad_ref, f32[3,1024,128]{2,1,0:T(8,128)} %broadcast_in_dim.94.masks_ref, f32[8,1024]{1,0:T(8,128)} %concatenate.20.taps_ref), custom_call_target="tpu_custom_call" | custom-call | flops 62914560 | bytes 10485760 | tf_op jit(solution)/shard_map/conv_backward/pallas_call | solution.py:287
  488.9 9.6 %convolution_convert_fusion = bf16[2048,1024]{1,0:T(8,128)(2,1)} fusion(bf16[1024,2048]{1,0:T(8,128)(2,1)} %interleave.2, bf16[1024,1024]{1,0:T(8,128)(2,1)} %get-tuple-element.163), kind=kOutput, calls=%fused_computation.2 | convolution fusion | flops 4297064448 | bytes 10485760 | tf_op jit(solution)/shard_map/dot_general | solution.py:24
  498.4 3.4 fusion.9
  502.1 7.1 %fusion.53 = f32[1024,2048]{1,0:T(8,128)} fusion(bf16[1024,1024]{1,0:T(8,128)(2,1)S(1)} %copy-done.27, bf16[2048,1024]{1,0:T(8,128)(2,1)S(1)} %bitcast.235), kind=kOutput, calls=%fused_computation.156 | convolution fusion | flops 4294967296 | bytes 14680064 | tf_op jit(solution)/shard_map/dot_general | solution.py:24
  509.2 9.2 %add_convert_fusion = bf16[1024,2048]{1,0:T(8,128)(2,1)} fusion(f32[1024,2048]{1,0:T(8,128)} %fusion.53, f32[1024,2048]{1,0:T(8,128)} %fusion.52), kind=kLoop, calls=%fused_computation.1 | loop fusion | flops 4194304 | bytes 20971520 | tf_op jit(solution)/shard_map/convert_element_type | solution.py:1324
  518.4 63.5 %scatter_all.1 = (bf16[4,256,1024]{2,1,0:T(8,128)(2,1)}, bf16[4,320,128]{2,1,0:T(8,128)(2,1)}, f32[256,2048]{1,0:T(8,128)}) custom-call(bf16[8,256,1024]{2,1,0:T(8,128)(2,1)} %bitcast.216, bf16[8,320,128]{2,1,0:T(8,128)(2,1)} %bitcast_bitcast_fusion.small_ref, bf16[4,256,2048]{2,1,0:T(8,128)(2,1)} %bitcast.204), custom_call_target="tpu_custom_call" | custom-call | bytes 8388608 | tf_op jit(solution)/shard_map/scatter_all/pallas_call | solution.py:678
  581.9 2.2 fusion.1
  586.8 6.9 %spread_columns.3 = (f32[256,8192]{1,0:T(8,128)}, f32[256,128]{1,0:T(8,128)}) custom-call(s32[1]{0:T(128)} %bitcast.80.copy_ref, bf16[256,1024]{1,0:T(8,128)(2,1)} %get-tuple-element.200.refs_0_, bf16[256,1024]{1,0:T(8,128)(2,1)} %get-tuple-element.199.refs_1_, bf16[256,1024]{1,0:T(8,128)(2,1)} %get-tuple-element.198.refs_2_, ...), custom_call_target="tpu_custom_call", output_to_operand_aliasing={{0}: (6, {})} | custom-call | flops 1048576 | bytes 5242880 | tf_op jit(solution)/shard_map/spread_columns/pallas_call | solution.py:1070
  595.3 1.6 gather_fusion
  598.7 1.5 fusion.39
  601.5 1.4 bitcast_bitcast_fusion.2
  602.9 1.7 bitcast_bitcast_fusion.1
  604.6 5.4 collective-permute-done.26
  610.0 1.5 convert_add_fusion.1
  611.5 2.1 fusion.4
  (219 shorter events, 57.0 us)
Async XLA Ops:
  0.6 94.3 %copy-start = (bf16[512,2048]{1,0:T(8,128)(2,1)S(1)}, bf16[512,2048]{1,0:T(8,128)(2,1)}, u32[]{:S(2)}) copy-start(bf16[512,2048]{1,0:T(8,128)(2,1)} %param.27) | copy-start | bytes 6291460
  91.8 79.6 %collective-permute-start = (bf16[256,1024]{1,0:T(8,128)(2,1)}, bf16[256,1024]{1,0:T(8,128)(2,1)S(1)}, u32[]{:S(2)}, u32[]{:S(2)}) collective-permute-start(bf16[256,1024]{1,0:T(8,128)(2,1)} %get-tuple-element.99), channel_id=1, source_target_pairs={{0,8},{8,16},{16,24},{24,28},{28,20},{20,12},{12,4},{4,0},{1,9},{9... | collective-permute-start | bytes 1572872 | tf_op jit(solution)/shard_map/ppermute | solution.py:67
  94.9 76.6 %collective-permute-start.1 = (bf16[256,1024]{1,0:T(8,128)(2,1)}, bf16[256,1024]{1,0:T(8,128)(2,1)}, u32[]{:S(2)}, u32[]{:S(2)}) collective-permute-start(bf16[256,1024]{1,0:T(8,128)(2,1)} %get-tuple-element.99), channel_id=1, source_target_pairs={{0,4},{8,0},{16,8},{24,16},{28,24},{20,28},{12,20},{4,12},{1,5},{9... | collective-permute-start | bytes 1572872 | tf_op jit(solution)/shard_map/ppermute | solution.py:70
  95.0 159.2 %collective-permute-start.11 = (bf16[128,2048]{1,0:T(8,128)(2,1)S(1)}, bf16[128,2048]{1,0:T(8,128)(2,1)}, u32[]{:S(2)}, u32[]{:S(2)}) collective-permute-start(bf16[128,2048]{1,0:T(8,128)(2,1)S(1)} %constant_dynamic-slice_fusion), channel_id=1, source_target_pairs={{0,8},{8,16},{16,24},{24,28},{28,20},{20,12},{12,4},{4,0},{1,9},{9... | collective-permute-start | bytes 1572872 | tf_op jit(solution)/shard_map/ppermute | solution.py:67
  97.0 157.1 %collective-permute-start.12 = (bf16[128,2048]{1,0:T(8,128)(2,1)S(1)}, bf16[128,2048]{1,0:T(8,128)(2,1)}, u32[]{:S(2)}, u32[]{:S(2)}) collective-permute-start(bf16[128,2048]{1,0:T(8,128)(2,1)S(1)} %constant_dynamic-slice_fusion), channel_id=1, source_target_pairs={{0,4},{8,0},{16,8},{24,16},{28,24},{20,28},{12,20},{4,12},{1,5},{9... | collective-permute-start | bytes 1572872 | tf_op jit(solution)/shard_map/ppermute | solution.py:70
  99.7 10.9 %copy-start.15 = (f32[320,1024]{1,0:T(8,128)}, f32[320,1024]{1,0:T(8,128)S(1)}, u32[]{:S(2)}) copy-start(f32[320,1024]{1,0:T(8,128)S(1)} %convert_element_type.115) | copy-start | bytes 3932164
  102.0 8.5 %copy-start.24 = (bf16[8,256,1024]{2,1,0:T(8,128)(2,1)S(1)}, bf16[8,256,1024]{2,1,0:T(8,128)(2,1)}, u32[]{:S(2)}) copy-start(bf16[8,256,1024]{2,1,0:T(8,128)(2,1)} %get-tuple-element.103) | copy-start | bytes 12582916
  110.6 15.2 %copy-start.6 = (bf16[320,1024]{1,0:T(8,128)(2,1)S(1)}, bf16[320,1024]{1,0:T(8,128)(2,1)}, u32[]{:S(2)}) copy-start(bf16[320,1024]{1,0:T(8,128)(2,1)} %get-tuple-element.101) | copy-start | bytes 1966084
  118.9 6.9 %copy-start.28 = (s32[8]{0:T(128)S(1)}, s32[8]{0:T(128)}, u32[]{:S(2)}) copy-start(s32[8]{0:T(128)} %constant.185.clone) | copy-start | bytes 100
  118.9 13.5 %copy-start.22 = (s32[8]{0:T(128)S(1)}, s32[8]{0:T(128)}, u32[]{:S(2)}) copy-start(s32[8]{0:T(128)} %constant.184.clone) | copy-start | bytes 100
  170.6 3.5 copy-start.19
  174.0 3.0 collective-permute-start.4
  174.9 14.6 %collective-permute-start.2 = (bf16[256,1024]{1,0:T(8,128)(2,1)S(1)}, bf16[256,1024]{1,0:T(8,128)(2,1)}, u32[]{:S(2)}, u32[]{:S(2)}) collective-permute-start(bf16[256,1024]{1,0:T(8,128)(2,1)S(1)} %collective-permute-done), channel_id=1, source_target_pairs={{0,8},{8,16},{16,24},{24,28},{28,20},{20,12},{12,4},{4,0},{1,9},{9... | collective-permute-start | bytes 1572872 | tf_op jit(solution)/shard_map/ppermute | solution.py:67
  176.9 14.3 %collective-permute-start.3 = (bf16[256,1024]{1,0:T(8,128)(2,1)}, bf16[256,1024]{1,0:T(8,128)(2,1)}, u32[]{:S(2)}, u32[]{:S(2)}) collective-permute-start(bf16[256,1024]{1,0:T(8,128)(2,1)} %collective-permute-done.1), channel_id=1, source_target_pairs={{0,4},{8,0},{16,8},{24,16},{28,24},{20,28},{12,20},{4,12},{1,5},{9... | collective-permute-start | bytes 1572872 | tf_op jit(solution)/shard_map/ppermute | solution.py:70
  177.1 9.8 %collective-permute-start.5 = (f32[2,256,160]{1,2,0:T(8,128)S(1)}, f32[2,256,160]{1,2,0:T(8,128)S(1)}, u32[]{:S(2)}, u32[]{:S(2)}) collective-permute-start(f32[2,256,160]{1,2,0:T(8,128)S(1)} %pad_maximum_fusion.4), channel_id=1, source_target_pairs={{0,2},{1,3},{2,0},{3,1},{4,6},{5,7},{6,4},{7,5},{8,10},{9,11},{10,... | collective-permute-start | bytes 983048 | tf_op jit(solution)/shard_map/ppermute | solution.py:164
  191.2 6.1 collective-permute-start.8
  191.3 29.5 %collective-permute-start.6 = (bf16[256,1024]{1,0:T(8,128)(2,1)}, bf16[256,1024]{1,0:T(8,128)(2,1)}, u32[]{:S(2)}, u32[]{:S(2)}) collective-permute-start(bf16[256,1024]{1,0:T(8,128)(2,1)} %collective-permute-done.2), channel_id=1, source_target_pairs={{0,8},{8,16},{16,24},{24,28},{28,20},{20,12},{12,4},{4,0},{1,9},{9... | collective-permute-start | bytes 1572872 | tf_op jit(solution)/shard_map/ppermute | solution.py:67
  193.0 27.9 %collective-permute-start.7 = (bf16[256,1024]{1,0:T(8,128)(2,1)}, bf16[256,1024]{1,0:T(8,128)(2,1)}, u32[]{:S(2)}, u32[]{:S(2)}) collective-permute-start(bf16[256,1024]{1,0:T(8,128)(2,1)} %collective-permute-done.3), channel_id=1, source_target_pairs={{0,4},{8,0},{16,8},{24,16},{28,24},{20,28},{12,20},{4,12},{1,5},{9... | collective-permute-start | bytes 1572872 | tf_op jit(solution)/shard_map/ppermute | solution.py:70
  221.8 22.6 %collective-permute-start.9 = (bf16[128,1024]{1,0:T(8,128)(2,1)S(1)}, bf16[128,1024]{1,0:T(8,128)(2,1)S(1)}, u32[]{:S(2)}, u32[]{:S(2)}) collective-permute-start(bf16[128,1024]{1,0:T(8,128)(2,1)S(1)} %slice.253), channel_id=1, source_target_pairs={{0,8},{8,16},{16,24},{24,28},{28,20},{20,12},{12,4},{4,0},{1,9},{9... | collective-permute-start | bytes 786440 | tf_op jit(solution)/shard_map/ppermute | solution.py:67
  224.4 20.1 %collective-permute-start.10 = (bf16[128,1024]{1,0:T(8,128)(2,1)S(1)}, bf16[128,1024]{1,0:T(8,128)(2,1)S(1)}, u32[]{:S(2)}, u32[]{:S(2)}) collective-permute-start(bf16[128,1024]{1,0:T(8,128)(2,1)S(1)} %slice.254), channel_id=1, source_target_pairs={{0,4},{8,0},{16,8},{24,16},{28,24},{20,28},{12,20},{4,12},{1,5},{9... | collective-permute-start | bytes 786440 | tf_op jit(solution)/shard_map/ppermute | solution.py:70
  226.8 19.1 %copy-start.8 = (bf16[1024,2048]{1,0:T(8,128)(2,1)S(1)}, bf16[1024,2048]{1,0:T(8,128)(2,1)}, u32[]{:S(2)}) copy-start(bf16[1024,2048]{1,0:T(8,128)(2,1)} %interleave.2) | copy-start | bytes 12582916
  254.2 14.1 %collective-permute-start.13 = (bf16[128,2048]{1,0:T(8,128)(2,1)}, bf16[128,2048]{1,0:T(8,128)(2,1)S(1)}, u32[]{:S(2)}, u32[]{:S(2)}) collective-permute-start(bf16[128,2048]{1,0:T(8,128)(2,1)} %collective-permute-done.11), channel_id=1, source_target_pairs={{0,8},{8,16},{16,24},{24,28},{28,20},{20,12},{12,4},{4,0},{1,9},{9... | collective-permute-start | bytes 1572872 | tf_op jit(solution)/shard_map/ppermute | solution.py:67
  255.7 13.2 %collective-permute-start.14 = (bf16[128,2048]{1,0:T(8,128)(2,1)}, bf16[128,2048]{1,0:T(8,128)(2,1)S(1)}, u32[]{:S(2)}, u32[]{:S(2)}) collective-permute-start(bf16[128,2048]{1,0:T(8,128)(2,1)} %collective-permute-done.12), channel_id=1, source_target_pairs={{0,4},{8,0},{16,8},{24,16},{28,24},{20,28},{12,20},{4,12},{1,5},{9... | collective-permute-start | bytes 1572872 | tf_op jit(solution)/shard_map/ppermute | solution.py:70
  268.9 13.1 %collective-permute-start.15 = (bf16[128,2048]{1,0:T(8,128)(2,1)S(1)}, bf16[128,2048]{1,0:T(8,128)(2,1)S(1)}, u32[]{:S(2)}, u32[]{:S(2)}) collective-permute-start(bf16[128,2048]{1,0:T(8,128)(2,1)S(1)} %collective-permute-done.13), channel_id=1, source_target_pairs={{0,8},{8,16},{16,24},{24,28},{28,20},{20,12},{12,4},{4,0},{1,9},{9... | collective-permute-start | bytes 1572872 | tf_op jit(solution)/shard_map/ppermute | solution.py:67
  270.5 11.8 %collective-permute-start.16 = (bf16[128,2048]{1,0:T(8,128)(2,1)S(1)}, bf16[128,2048]{1,0:T(8,128)(2,1)S(1)}, u32[]{:S(2)}, u32[]{:S(2)}) collective-permute-start(bf16[128,2048]{1,0:T(8,128)(2,1)S(1)} %collective-permute-done.14), channel_id=1, source_target_pairs={{0,4},{8,0},{16,8},{24,16},{28,24},{20,28},{12,20},{4,12},{1,5},{9... | collective-permute-start | bytes 1572872 | tf_op jit(solution)/shard_map/ppermute | solution.py:70
  280.4 12.5 %copy-start.11 = (bf16[1024,2048]{1,0:T(8,128)(2,1)S(1)}, bf16[1024,2048]{1,0:T(8,128)(2,1)}, u32[]{:S(2)}) copy-start(bf16[1024,2048]{1,0:T(8,128)(2,1)} %interleave.3) | copy-start | bytes 12582916
  283.1 6.4 %collective-permute-start.17 = (bf16[64,2048]{1,0:T(8,128)(2,1)S(1)}, bf16[64,2048]{1,0:T(8,128)(2,1)S(1)}, u32[]{:S(2)}, u32[]{:S(2)}) collective-permute-start(bf16[64,2048]{1,0:T(8,128)(2,1)S(1)} %slice.255), channel_id=1, source_target_pairs={{0,8},{8,16},{16,24},{24,28},{28,20},{20,12},{12,4},{4,0},{1,9},{9... | collective-permute-start | bytes 786440 | tf_op jit(solution)/shard_map/ppermute | solution.py:67
  284.6 6.8 %collective-permute-start.18 = (bf16[64,2048]{1,0:T(8,128)(2,1)S(1)}, bf16[64,2048]{1,0:T(8,128)(2,1)S(1)}, u32[]{:S(2)}, u32[]{:S(2)}) collective-permute-start(bf16[64,2048]{1,0:T(8,128)(2,1)S(1)} %slice.256), channel_id=1, source_target_pairs={{0,4},{8,0},{16,8},{24,16},{28,24},{20,28},{12,20},{4,12},{1,5},{9... | collective-permute-start | bytes 786440 | tf_op jit(solution)/shard_map/ppermute | solution.py:70
  413.9 37.5 %collective-permute-start.21 = (bf16[128,2048]{1,0:T(8,128)(2,1)}, bf16[128,2048]{1,0:T(8,128)(2,1)}, u32[]{:S(2)}, u32[]{:S(2)}) collective-permute-start(bf16[128,2048]{1,0:T(8,128)(2,1)} %get-tuple-element.182.refs_0_), channel_id=1, source_target_pairs={{0,1},{1,0},{2,3},{3,2},{4,5},{5,4},{6,7},{7,6},{8,9},{9,8},{10,11... | collective-permute-start | bytes 1572872 | tf_op jit(solution)/shard_map/ppermute | solution.py:164
  413.9 28.9 %collective-permute-start.22 = (bf16[128,2048]{1,0:T(8,128)(2,1)}, bf16[128,2048]{1,0:T(8,128)(2,1)}, u32[]{:S(2)}, u32[]{:S(2)}) collective-permute-start(bf16[128,2048]{1,0:T(8,128)(2,1)} %get-tuple-element.182.refs_0_), channel_id=1, source_target_pairs={{0,2},{1,3},{2,0},{3,1},{4,6},{5,7},{6,4},{7,5},{8,10},{9,11},{10,... | collective-permute-start | bytes 1572872 | tf_op jit(solution)/shard_map/ppermute | solution.py:164
  415.5 42.4 %collective-permute-start.27 = (bf16[256,1024]{1,0:T(8,128)(2,1)}, bf16[256,1024]{1,0:T(8,128)(2,1)}, u32[]{:S(2)}, u32[]{:S(2)}) collective-permute-start(bf16[256,1024]{1,0:T(8,128)(2,1)} %get-tuple-element.176.refs_0_), channel_id=1, source_target_pairs={{0,1},{1,0},{2,3},{3,2},{4,5},{5,4},{6,7},{7,6},{8,9},{9,8},{10,11... | collective-permute-start | bytes 1572872 | tf_op jit(solution)/shard_map/ppermute | solution.py:164
  415.7 27.9 %collective-permute-start.28 = (bf16[256,1024]{1,0:T(8,128)(2,1)}, bf16[256,1024]{1,0:T(8,128)(2,1)}, u32[]{:S(2)}, u32[]{:S(2)}) collective-permute-start(bf16[256,1024]{1,0:T(8,128)(2,1)} %get-tuple-element.176.refs_0_), channel_id=1, source_target_pairs={{0,2},{1,3},{2,0},{3,1},{4,6},{5,7},{6,4},{7,5},{8,10},{9,11},{10,... | collective-permute-start | bytes 1572872 | tf_op jit(solution)/shard_map/ppermute | solution.py:164
  421.2 19.8 %collective-permute-start.19 = (f32[2,256,160]{1,2,0:T(8,128)S(1)}, f32[2,256,160]{1,2,0:T(8,128)S(1)}, u32[]{:S(2)}, u32[]{:S(2)}) collective-permute-start(f32[2,256,160]{1,2,0:T(8,128)S(1)} %pad_maximum_fusion.5), channel_id=1, source_target_pairs={{0,1},{1,0},{2,3},{3,2},{4,5},{5,4},{6,7},{7,6},{8,9},{9,8},{10,11... | collective-permute-start | bytes 983048 | tf_op jit(solution)/shard_map/ppermute | solution.py:164
  422.0 7.5 %copy-start.26 = (bf16[1024,1024]{1,0:T(8,128)(2,1)S(1)}, bf16[1024,1024]{1,0:T(8,128)(2,1)}, u32[]{:S(2)}) copy-start(bf16[1024,1024]{1,0:T(8,128)(2,1)} %get-tuple-element.159) | copy-start | bytes 6291460
  429.4 22.0 %copy-start.9 = (bf16[1024,2048]{1,0:T(8,128)(2,1)}, bf16[1024,2048]{1,0:T(8,128)(2,1)S(1)}, u32[]{:S(2)}) copy-start(bf16[1024,2048]{1,0:T(8,128)(2,1)S(1)} %convolution_convert_fusion.1) | copy-start | bytes 12582916
  429.5 10.5 %copy-start.16 = (f32[18,8,1024]{2,1,0:T(8,128)S(1)}, f32[18,8,1024]{2,1,0:T(8,128)}, u32[]{:S(2)}) copy-start(f32[18,8,1024]{2,1,0:T(8,128)} %get-tuple-element.166) | copy-start | bytes 1769476
  429.5 13.6 %copy-start.3 = (bf16[1024,1024]{1,0:T(8,128)(2,1)S(1)}, bf16[1024,1024]{1,0:T(8,128)(2,1)}, u32[]{:S(2)}) copy-start(bf16[1024,1024]{1,0:T(8,128)(2,1)} %get-tuple-element.154) | copy-start | bytes 6291460
  441.2 10.1 %collective-permute-start.20 = (f32[2,256,160]{1,2,0:T(8,128)S(1)}, f32[2,256,160]{1,2,0:T(8,128)S(1)}, u32[]{:S(2)}, u32[]{:S(2)}) collective-permute-start(f32[2,256,160]{1,2,0:T(8,128)S(1)} %pad_maximum_fusion.6), channel_id=1, source_target_pairs={{0,2},{1,3},{2,0},{3,1},{4,6},{5,7},{6,4},{7,5},{8,10},{9,11},{10,... | collective-permute-start | bytes 983048 | tf_op jit(solution)/shard_map/ppermute | solution.py:164
  442.8 8.6 %collective-permute-start.23 = (bf16[128,2048]{1,0:T(8,128)(2,1)}, bf16[128,2048]{1,0:T(8,128)(2,1)S(1)}, u32[]{:S(2)}, u32[]{:S(2)}) collective-permute-start(bf16[128,2048]{1,0:T(8,128)(2,1)} %collective-permute-done.22.refs_2_), channel_id=1, source_target_pairs={{0,1},{1,0},{2,3},{3,2},{4,5},{5,4},{6,7},{7,6},{8,9},{9,8},{10,11... | collective-permute-start | bytes 1572872 | tf_op jit(solution)/shard_map/ppermute | solution.py:164
  443.5 14.4 %collective-permute-start.29 = (bf16[256,1024]{1,0:T(8,128)(2,1)}, bf16[256,1024]{1,0:T(8,128)(2,1)S(1)}, u32[]{:S(2)}, u32[]{:S(2)}) collective-permute-start(bf16[256,1024]{1,0:T(8,128)(2,1)} %collective-permute-done.28.refs_2_), channel_id=1, source_target_pairs={{0,1},{1,0},{2,3},{3,2},{4,5},{5,4},{6,7},{7,6},{8,9},{9,8},{10,11... | collective-permute-start | bytes 1572872 | tf_op jit(solution)/shard_map/ppermute | solution.py:164
  451.4 1.8 copy-start.18
  451.4 14.4 %collective-permute-start.24 = (bf16[2,256,160]{1,2,0:T(8,128)(2,1)S(1)}, bf16[2,256,160]{1,2,0:T(8,128)(2,1)S(1)}, u32[]{:S(2)}, u32[]{:S(2)}) collective-permute-start(bf16[2,256,160]{1,2,0:T(8,128)(2,1)S(1)} %fusion.79), channel_id=1, source_target_pairs={{0,1},{1,0},{2,3},{3,2},{4,5},{5,4},{6,7},{7,6},{8,9},{9,8},{10,11... | collective-permute-start | bytes 491528 | tf_op jit(solution)/shard_map/ppermute | solution.py:164
  453.2 45.2 %collective-permute-start.25 = (bf16[2,256,2048]{2,1,0:T(8,128)(2,1)}, bf16[2,256,2048]{2,1,0:T(8,128)(2,1)}, u32[]{:S(2)}, u32[]{:S(2)}) collective-permute-start(bf16[2,256,2048]{2,1,0:T(8,128)(2,1)} %pad_maximum_fusion), channel_id=1, source_target_pairs={{0,1},{1,0},{2,3},{3,2},{4,5},{5,4},{6,7},{7,6},{8,9},{9,8},{10,11... | collective-permute-start | bytes 6291464 | tf_op jit(solution)/shard_map/ppermute | solution.py:164
  457.9 0.8 copy-start.17
  466.8 2.2 copy-start.7
  471.9 15.0 %copy-start.4 = (bf16[1024,1024]{1,0:T(8,128)(2,1)S(1)}, bf16[1024,1024]{1,0:T(8,128)(2,1)}, u32[]{:S(2)}) copy-start(bf16[1024,1024]{1,0:T(8,128)(2,1)} %get-tuple-element.110) | copy-start | bytes 6291460
  488.9 9.6 %copy-start.10 = (bf16[1024,2048]{1,0:T(8,128)(2,1)S(1)}, bf16[1024,2048]{1,0:T(8,128)(2,1)}, u32[]{:S(2)}) copy-start(bf16[1024,2048]{1,0:T(8,128)(2,1)} %copy-done.9) | copy-start | bytes 12582916
  498.4 3.4 copy-start.25
  498.4 3.6 copy-start.27
  518.4 63.5 %copy-start.2 = (bf16[2,128,2048]{2,1,0:T(8,128)(2,1)S(1)}, bf16[2,128,2048]{2,1,0:T(8,128)(2,1)}, u32[]{:S(2)}) copy-start(bf16[2,128,2048]{2,1,0:T(8,128)(2,1)} %refs_2_.1) | copy-start | bytes 3145732
  518.4 63.5 %copy-start.21 = (f32[2,1024]{1,0:T(2,128)S(1)}, f32[2,1024]{1,0:T(2,128)}, u32[]{:S(2)}) copy-start(f32[2,1024]{1,0:T(2,128)} %slice.299) | copy-start | bytes 24580
  581.9 3.6 copy-start.14
  584.1 25.9 %collective-permute-start.26 = (bf16[256,2048]{1,0:T(8,128)(2,1)}, bf16[256,2048]{1,0:T(8,128)(2,1)}, u32[]{:S(2)}, u32[]{:S(2)}) collective-permute-start(bf16[256,2048]{1,0:T(8,128)(2,1)} %get-tuple-element.169), channel_id=1, source_target_pairs={{0,2},{1,3},{2,0},{3,1},{4,6},{5,7},{6,4},{7,5},{8,10},{9,11},{10,... | collective-permute-start | bytes 3145736 | tf_op jit(solution)/shard_map/ppermute | solution.py:164
  586.8 6.9 %copy-start.20 = (f32[256,128]{1,0:T(8,128)S(1)}, f32[256,128]{1,0:T(8,128)}, u32[]{:S(2)}) copy-start(f32[256,128]{1,0:T(8,128)} %get-tuple-element.179) | copy-start | bytes 393220
  586.8 7.9 %copy-start.23 = (bf16[256]{0:T(256)(128)(2,1)S(1)}, bf16[256]{0:T(256)(128)(2,1)}, u32[]{:S(2)}) copy-start(bf16[256]{0:T(256)(128)(2,1)} %param.18) | copy-start | bytes 1540
  597.0 0.8 copy-start.13
  598.7 12.9 %copy-start.5 = (f32[256,2048]{1,0:T(8,128)S(1)}, f32[256,2048]{1,0:T(8,128)}, u32[]{:S(2)}) copy-start(f32[256,2048]{1,0:T(8,128)} %get-tuple-element.174) | copy-start | bytes 6291460
  598.7 12.9 %copy-start.12 = (bf16[2,128,2048]{2,1,0:T(8,128)(2,1)S(1)}, bf16[2,128,2048]{2,1,0:T(8,128)(2,1)}, u32[]{:S(2)}) copy-start(bf16[2,128,2048]{2,1,0:T(8,128)(2,1)} %refs_3_.1) | copy-start | bytes 3145732
  611.5 2.2 copy-start.1
where the time goes:
time: 623 us; the launch traced here: 614 us
  Pallas kernels  351 us (56%)
  matrix products  86 us (14%)
  local copies, waits for them, and re-layouts  60.4 us (10%)
  other arithmetic  36.1 us (6%)
  waiting for transfers between devices  28.1 us (5%)
  starting transfers between devices  26.7 us (4%)
  between operations  25.5 us (4%)
    pallas_call x1, Pallas kernels, scan_backward(): pl.pallas_call(functools.partial(scan_back_kernel, nstate, chunk, rings),...  94 us
    dot_general x15, matrix products, dot(): lax.dot_general(left, right, (((left_dim,), (right_dim,)), ((), ())), pre...  86 us
    pallas_call x1, Pallas kernels, gather_all(): pl.pallas_call(kernel, in_specs=[anywhere] * (2 + count), out_specs=[anyw...  84.9 us
    pallas_call x1, Pallas kernels, scatter_all(): pl.pallas_call(functools.partial(scatter_kernel, size), in_specs=[inside]...  63.5 us
    pallas_call x2, Pallas kernels, scan_forward(): pl.pallas_call(functools.partial(scan_kernel, nstate, 256), grid=(count,)...  31.3 us
    dynamic_update_slice x18, local copies, waits for them, and re-layouts, put(): self.whole = lax.dynamic_update_slice(self.whole, piece[None], at)  22 us
    ppermute x14, waiting for transfers between devices, swap(): return lax.ppermute(value, 'rep', [(r, r ^ bit) for r in range(COPIES)])  17.9 us
    pallas_call x2, Pallas kernels, interleave(): pl.pallas_call(functools.partial(rows_kernel, gain is not None), grid=(le...  16.4 us
  transfers between devices with their start and end apart: 30, of which 9 were waited for; matrix products, arithmetic and copies ran while one was open for 21% of the time, Pallas kernels for 16%

commit v1 on v0

--- a/solution.py
+++ b/solution.py
@@ -233,11 +233,11 @@
         ].astype(out_ref.dtype)
 
 
-def conv_kernel(inner_ref, masks_ref, taps_ref, act_ref, low_ref, held):
+def conv_kernel(inner_ref, masks_ref, taps_ref, act_ref, low_ref):
     value = conv_of(inner_ref[...], masks_ref, taps_ref[...])
     act = value * sigmoid(value)
     act_ref[...] = act
-    by_sequence(held, low_ref, act)
+    low_ref[...] = act.astype(BF16)
 
 
 def conv_forward(inner, masks, taps):
@@ -256,7 +256,6 @@
             jax.ShapeDtypeStruct((rows, width), F32),
             jax.ShapeDtypeStruct((rows, width), BF16),
         ],
-        scratch_shapes=[pltpu.VMEM((rows, LANES), F32)],
         compiler_params=params(),
         cost_estimate=cost(30 * rows * width, 10 * rows * width),
         name="conv_forward",
@@ -415,140 +414,6 @@
         device_id=peer,
         device_id_type=pl.DeviceIdType.MESH,
     )
-
-
-def gather_kernel(
-    size, entry_ref, few_ref, own_refs, whole_ref, gate_ref, all_ref, copies_refs, inner_ref, local, ring_sems, few_sems, rep_sems
-):
-    peers = Peers(size)
-    half = peers.half
-    rows, few_rows = inner_ref.shape[0] // 2, few_ref.shape[0] // 2
-    keep = []
-    for f in range(size):
-        for side, target in enumerate((inner_ref, gate_ref)):
-            source = ((side * size + f) * COPIES + peers.copy) * LANES
-            keep.append(
-                pltpu.make_async_copy(
-                    entry_ref.at[:, pl.ds(pl.multiple_of(source, LANES), LANES)],
-                    target.at[:, pl.ds(f * LANES, LANES)],
-                    local.at[len(keep)],
-                )
-            )
-    for copy in keep:
-        copy.start()
-    peers.meet()
-    for copy in keep:
-        copy.wait()
-
-    sent = []
-
-    def start(*copy):
-        moving = remote(*copy)
-        moving.start()
-        sent.append(moving)
-
-    for i, (own, copies) in enumerate(zip(own_refs, copies_refs)):
-        start(own, copies.at[2], rep_sems, (i, 0), peers.across)
-        start(own, copies.at[1], rep_sems, (i, 1), peers.core)
-
-    def chunk(ref, c, step, n):
-        return ref.at[pl.ds(c * n, n), :]
-
-    def owner(way, step):
-        return peers.at(-step if way == 0 else step)
-
-    def come(way, step, c):
-        piece = chunk(whole_ref.at[owner(way, step)], c, step, rows)
-        remote(piece, piece, ring_sems, (way, step - 1, c), peers.ring[way]).wait_recv()
-
-    def few_piece(way, step, last):
-        columns = pl.ds(pl.multiple_of(owner(way, step) * LANES, LANES), LANES)
-        return all_ref.at[pl.ds(way * few_rows if last else 0, few_rows * (1 if last else 2)), columns]
-
-    def few_come(way, step):
-        piece = few_piece(way, step, step == half)
-        remote(piece, piece, few_sems, (way, step - 1), peers.ring[way]).wait_recv()
-
-    for step in range(1, half + 1):
-        last = step == half
-        for way in range(2):
-            if step > 1:
-                few_come(way, step - 1)
-            target = few_piece(way, step - 1, last)
-            source = few_ref if step == 1 else target
-            start(source, target, few_sems, (way, step - 1), peers.ring[way])
-        for c in range(2):
-            for way in range(2):
-                if last and c != way:
-                    continue
-                if step > 1:
-                    come(way, step - 1, c)
-                target = chunk(whole_ref.at[owner(way, step - 1)], c, step, rows)
-                source = chunk(inner_ref, c, step, rows) if step == 1 else target
-                start(source, target, ring_sems, (way, step - 1, c), peers.ring[way])
-        if step == 1:
-            mine = pl.ds(pl.multiple_of(peers.member * LANES, LANES), LANES)
-            keep = [
-                pltpu.make_async_copy(inner_ref, whole_ref.at[peers.member], local.at[0]),
-                pltpu.make_async_copy(few_ref, all_ref.at[:, mine], local.at[1]),
-            ]
-            for i, (own, copies) in enumerate(zip(own_refs, copies_refs)):
-                keep.append(pltpu.make_async_copy(own, copies.at[0], local.at[2 + i]))
-            for copy in keep:
-                copy.start()
-    for i, copies in enumerate(copies_refs):
-        remote(copies.at[2], copies.at[2], rep_sems, (i, 0), peers.across).wait_recv()
-        start(copies.at[2], copies.at[3], rep_sems, (i, 2), peers.core)
-    for way in range(2):
-        come(way, half - 1, 1 - way)
-        come(way, half, way)
-        few_come(way, half)
-    for i, copies in enumerate(copies_refs):
-        remote(copies.at[1], copies.at[1], rep_sems, (i, 1), peers.core).wait_recv()
-        remote(copies.at[3], copies.at[3], rep_sems, (i, 2), peers.core).wait_recv()
-    for moving in sent:
-        moving.wait_send()
-    for copy in keep:
-        copy.wait()
-
-
-def gather_all(size, entry, few, own):
-    anywhere = pl.BlockSpec(memory_space=pl.ANY)
-    count, half = len(own), size // 2
-    shard = (entry.shape[0], size * LANES)
-
-    def kernel(*refs):
-        entry_ref, few_ref = refs[:2]
-        own_refs = refs[2 : 2 + count]
-        whole_ref, gate_ref, all_ref = refs[2 + count : 5 + count]
-        copies_refs = refs[5 + count : 5 + 2 * count]
-        inner_ref, local, *sems = refs[5 + 2 * count :]
-        pairs = [sems[i : i + 2] for i in range(0, 6, 2)]
-        gather_kernel(
-            size, entry_ref, few_ref, own_refs, whole_ref, gate_ref, all_ref, copies_refs, inner_ref, local, *pairs
-        )
-
-    ring_sems = pltpu.SemaphoreType.DMA((2, half, 2))
-    few_sems = pltpu.SemaphoreType.DMA((2, half))
-    rep_sems = pltpu.SemaphoreType.DMA((count, 3))
-    outs = [
-        jax.ShapeDtypeStruct((size,) + shard, entry.dtype),
-        jax.ShapeDtypeStruct(shard, entry.dtype),
-        jax.ShapeDtypeStruct((few.shape[0], size * LANES), few.dtype),
-    ] + [jax.ShapeDtypeStruct((COPIES,) + o.shape, o.dtype) for o in own]
-    return pl.pallas_call(
-        kernel,
-        in_specs=[anywhere] * (2 + count),
-        out_specs=[anywhere] * (3 + count),
-        out_shape=outs,
-        scratch_shapes=[pltpu.VMEM(shard, entry.dtype), pltpu.SemaphoreType.DMA((2 * size,))]
-        + [ring_sems] * 2
-        + [few_sems] * 2
-        + [rep_sems] * 2,
-        compiler_params=pltpu.CompilerParams(collective_id=1, has_side_effects=True),
-        cost_estimate=cost(0, 4 * size * shard[0] * shard[1]),
-        name="gather_all",
-    )(entry, few, *own)
 
 
 def scatter_kernel(
@@ -734,14 +599,14 @@
 
 
 def scan_kernel(
-    nstate, chunk, pre_ref, act_ref, coef_ref, spread_ref, keep_ref, rate_ref, row_ref, held_ref, *refs
+    nstate, chunk, pre_ref, act_ref, coef_ref, spread_ref, keep_ref, rate_ref, row_ref,
+    out_ref, step_ref, start_ref, carry_ref, wide,
 ):
-    out_ref, step_ref, start_ref, carry_ref, wide = refs[-5:]
     width = pre_ref.shape[1]
 
     @pl.when(pl.program_id(0) == 0)
     def _():
-        carry_ref[...] = held_ref[...]
+        carry_ref[...] = jnp.zeros_like(carry_ref)
 
     start_ref[0] = carry_ref[...]
     wide[...] = jnp.dot(coef_ref[...], spread_ref[...], preferred_element_type=F32)
@@ -772,14 +637,15 @@
             carry_ref[n, :, cols] = states[n]
 
 
-def scan_forward(pre, act, coef, spread_by, keep, rate, rows, held, before, first, count):
+def scan_forward(pre, act, coef, spread_by, keep, rate, rows):
     total, width = pre.shape
     nstate = rate.shape[0]
     size = BLOCK * GROUP
-    tile = pl.BlockSpec((size, width), lambda t: (first + t, 0))
-    thin = pl.BlockSpec((size, LANES), lambda t: (first + t, 0))
+    tile = pl.BlockSpec((size, width), lambda t: (t, 0))
+    thin = pl.BlockSpec((size, LANES), lambda t: (t, 0))
     state = pl.BlockSpec((nstate, GROUP, width), lambda t: (0, 0, 0))
-    work = count * size * width * nstate
+    count = total // size
+    work = total * width * nstate
     return pl.pallas_call(
         functools.partial(scan_kernel, nstate, 256),
         grid=(count,),
@@ -791,27 +657,624 @@
             thin,
             state,
             pl.BlockSpec((8, width), lambda t: (0, 0)),
-            state,
-        ]
-        + [pl.BlockSpec(memory_space=pl.ANY)] * len(before),
+        ],
         out_specs=[
             tile,
             tile,
-            pl.BlockSpec((1, nstate, GROUP, width), lambda t: (first + t, 0, 0, 0)),
-            state,
+            pl.BlockSpec((1, nstate, GROUP, width), lambda t: (t, 0, 0, 0)),
         ],
         out_shape=[
             jax.ShapeDtypeStruct((total, width), F32),
             jax.ShapeDtypeStruct((total, width), F32),
             jax.ShapeDtypeStruct((total // size, nstate, GROUP, width), F32),
-            jax.ShapeDtypeStruct((nstate, GROUP, width), F32),
         ],
-        scratch_shapes=[pltpu.VMEM((size, 2 * nstate * LANES), F32)],
-        input_output_aliases={8 + i: i for i in range(len(before))},
+        scratch_shapes=[
+            pltpu.VMEM((nstate, GROUP, width), F32),
+            pltpu.VMEM((size, 2 * nstate * LANES), F32),
+        ],
         compiler_params=params(),
         cost_estimate=cost(16 * work, 16 * count * size * width),
         name="scan_forward",
-    )(pre, act, coef, spread_by, keep, rate, rows, held, *before)
+    )(pre, act, coef, spread_by, keep, rate, rows)
+
+
+class Shares:
+    def __init__(self, peers, shards, wholes, sems):
+        self.peers, self.shards, self.wholes, self.sems = peers, shards, wholes, sems
+        self.sent = []
+
+    def place(self, which, member, c):
+        rows = self.shards[which].shape[0]
+        start = pl.multiple_of(member * rows + c * (rows // 2), rows // 2)
+        return self.wholes[which].at[pl.ds(start, rows // 2), :]
+
+    def owner(self, way, step):
+        return self.peers.at(-step if way == 0 else step)
+
+    def chunks(self, way, step):
+        return (way,) if step == self.peers.half else (0, 1)
+
+    def come(self, which, way, step, c):
+        there = self.place(which, self.owner(way, step), c)
+        remote(there, there, self.sems, (which, way, step - 1, c), self.peers.ring[way]).wait_recv()
+
+    def step(self, which, step):
+        for c in range(2):
+            for way in range(2):
+                if c not in self.chunks(way, step):
+                    continue
+                target = self.place(which, self.owner(way, step - 1), c)
+                source = target
+                if step == 1:
+                    rows = self.shards[which].shape[0] // 2
+                    source = self.shards[which].at[pl.ds(c * rows, rows), :]
+                else:
+                    self.come(which, way, step - 1, c)
+                index = (which, way, step - 1, c)
+                remote(source, target, self.sems, index, self.peers.ring[way]).start()
+
+    def finish(self, which):
+        half = self.peers.half
+        for way in range(2):
+            self.come(which, way, half - 1, 1 - way)
+            self.come(which, way, half, way)
+
+    def sent_all(self):
+        for which in range(len(self.shards)):
+            for step in range(1, self.peers.half + 1):
+                for way in range(2):
+                    for c in self.chunks(way, step):
+                        place = self.place(which, self.owner(way, step - 1), c)
+                        index = (which, way, step - 1, c)
+                        remote(place, place, self.sems, index, self.peers.ring[way]).wait_send()
+
+
+def softplus(value):
+    return jnp.maximum(value, 0.0) + jnp.log1p(jnp.exp(-jnp.abs(value)))
+
+
+def forward_kernel(
+    size, rank, nstate,
+    entry, few, tokens, out_grad, segments, out_proj,
+    few_out, masks_out, rate_out, spread_out, fold_out, normed_out, cotangent_out, tokens_all, grads_all, segments_all,
+    w_in_out, inner_out, act_out, low_out, step_low_out, coef_out, step_out, start_out, gate_out, readout_out,
+    gated_out, natural_out, gate_w_out, out_w_out,
+    few_all, small, masks, rate, spread_by, fold_by, normed, stage, cotangent, held, seg, inner_shard, gate_shard, w_in,
+    inner, act, low, part, nat, got_near, to_across, got_across, shared, step_low, coef, wide, pre, step, readout,
+    carry, start_at, gate, gated, natural, gate_w,
+    local, start_sems, gate_sems, own_sems, entry_sems, stage_sems, out_sems, seg_sems,
+    ring_send, ring_recv, few_send, few_recv, rep_send, rep_recv, near_send, near_recv,
+):
+    peers = Peers(size)
+    total, width = normed.shape[0], w_in.shape[1]
+    pad = 3 * GROUP
+    chunk = 256
+    rows = 64
+    length = total // GROUP
+    batches = GROUP // COPIES
+    half = peers.half
+    side_rows = total // COPIES
+    saved = []
+
+    def save(source, target):
+        copy = pltpu.make_async_copy(source, target, local.at[len(saved)])
+        copy.start()
+        saved.append(copy)
+
+    picks = []
+    for side_of, target in enumerate((inner_shard, gate_shard)):
+        for f in range(size):
+            source = ((side_of * size + f) * COPIES + peers.copy) * LANES
+            picks.append(
+                pltpu.make_async_copy(
+                    entry.at[:, pl.ds(pl.multiple_of(source, LANES), LANES)],
+                    target.at[:, pl.ds(f * LANES, LANES)],
+                    entry_sems.at[len(picks)],
+                )
+            )
+    for pick in picks:
+        pick.start()
+    peers.meet()
+    sent = []
+
+    def send(*copy):
+        moving = remote(*copy)
+        moving.start()
+        sent.append(moving)
+
+    rep_sems = (rep_send, rep_recv)
+
+    def of_copy(ref, k):
+        return ref.at[k] if ref is segments_all else ref.at[pl.ds(k * batches, batches)]
+
+    def exchange(i, own, everyone):
+        send(own, of_copy(everyone, 2), rep_sems, (i, 0), peers.across)
+        send(own, of_copy(everyone, 1), rep_sems, (i, 1), peers.core)
+        copy = pltpu.make_async_copy(own, of_copy(everyone, 0), own_sems.at[3 + i])
+        copy.start()
+        return copy
+
+    def pass_on(i, everyone):
+        far = of_copy(everyone, 2)
+        remote(far, far, rep_sems, (i, 0), peers.across).wait_recv()
+        send(far, of_copy(everyone, 3), rep_sems, (i, 2), peers.core)
+
+    def exchanged(i, everyone, copy):
+        copy.wait()
+        for k, which in ((1, 1), (3, 2)):
+            there = of_copy(everyone, k)
+            remote(there, there, rep_sems, (i, which), peers.core).wait_recv()
+
+    out_rows = out_proj.shape[0] // COPIES
+    out_shard = out_proj.at[pl.ds(pl.multiple_of(peers.copy * out_rows, out_rows), out_rows), :]
+    ring = Shares(
+        peers, (inner_shard, gate_shard, out_shard), (w_in, gate_w, out_w_out), (ring_send, ring_recv),
+    )
+    gate_rows = gate_shard.shape[0]
+    shard_rows = pl.ds(pl.multiple_of(peers.member * gate_rows, gate_rows), gate_rows)
+    own_rows = pl.ds(pl.multiple_of(peers.member * out_rows, out_rows), out_rows)
+    own_columns = pl.ds(pl.multiple_of(peers.member * LANES, LANES), LANES)
+
+    few_sems = (few_send, few_recv)
+    few_rows = few.shape[0] // 2
+
+    def few_place(way, number, split):
+        columns = pl.ds(pl.multiple_of(ring.owner(way, number) * LANES, LANES), LANES)
+        place = pl.ds(way * few_rows, few_rows) if split else pl.ds(0, 2 * few_rows)
+        return few_all.at[place, columns]
+
+    def few_come(way, number):
+        there = few_place(way, number, number == half)
+        remote(there, there, few_sems, (way, number - 1), peers.ring[way]).wait_recv()
+
+    def few_step(number):
+        for way in range(2):
+            if number > 1:
+                few_come(way, number - 1)
+            target = few_place(way, number - 1, number == half)
+            source = few if number == 1 else target
+            send(source, target, few_sems, (way, number - 1), peers.ring[way])
+
+    few_step(1)
+    own_tokens = exchange(0, tokens, tokens_all)
+    own_segments = exchange(2, segments, segments_all)
+    own = [
+        pltpu.make_async_copy(few, few_all.at[:, own_columns], own_sems.at[0]),
+        pltpu.make_async_copy(out_shard, out_w_out.at[own_rows, :], own_sems.at[1]),
+    ]
+    for copy in own:
+        copy.start()
+    for pick in picks[:size]:
+        pick.wait()
+    ring.step(0, 1)
+    for pick in picks[size:]:
+        pick.wait()
+    own_shards = [
+        pltpu.make_async_copy(inner_shard, w_in.at[shard_rows, :], own_sems.at[6]),
+        pltpu.make_async_copy(gate_shard, gate_w.at[shard_rows, :], own_sems.at[2]),
+    ]
+    for copy in own_shards:
+        copy.start()
+
+    wide_shape, thin_shape = spread_by.shape, fold_by.shape
+    tile = lax.broadcasted_iota(jnp.int32, wide_shape, 1) // LANES
+    row = lax.broadcasted_iota(jnp.int32, wide_shape, 0)
+    spread_by[...] = jnp.where(
+        (lax.rem(row, 2 * nstate) == tile) & (row < 6 * nstate), 1.0, 0.0
+    ).astype(BF16)
+    tile = lax.broadcasted_iota(jnp.int32, thin_shape, 0) // LANES
+    column = lax.broadcasted_iota(jnp.int32, thin_shape, 1)
+    fold_by[...] = jnp.where(tile == column, 1.0, 0.0).astype(BF16)
+    save(spread_by, spread_out)
+    save(fold_by, fold_out)
+
+    few_step(2)
+    pass_on(2, segments_all)
+    few_step(3)
+    ring.step(0, 2)
+    few_step(4)
+    exchanged(2, segments_all, own_segments)
+    numbers = pltpu.make_async_copy(segments_all, seg, seg_sems.at[0])
+    numbers.start()
+    for way in range(2):
+        few_come(way, half - 1) if half < 2 else None
+        few_come(way, half)
+    own[0].wait()
+    numbers.wait()
+
+    numbers = jnp.concatenate([seg[k] for k in range(COPIES)], axis=0).astype(F32)
+    lane = lax.broadcasted_iota(jnp.int32, (total, LANES), 1)
+    time = lax.broadcasted_iota(jnp.int32, (total, LANES), 0) // GROUP
+    picked = jnp.where(lane == time, jnp.concatenate([numbers] * length, axis=0), 0.0).astype(BF16)
+    numbers = jnp.dot(picked, jnp.ones((LANES, LANES), BF16), preferred_element_type=F32)
+    for shift in range(1, 4):
+        earlier = jnp.concatenate(
+            [jnp.full((shift * GROUP, LANES), -1.0, F32), numbers[: -shift * GROUP]], axis=0
+        )
+        masks[shift - 1] = jnp.where(earlier == numbers, 1.0, 0.0)
+    save(masks, masks_out)
+    save(few_all, few_out)
+    first_small = 2 * rank + 2 * nstate
+    small[...] = few_all[first_small : first_small + small.shape[0], :].astype(F32)
+    taps, bias_row, skip_row, gain_row = 0, 5, 6 + nstate, 7 + nstate
+    for n in range(nstate):
+        rate[n] = jnp.broadcast_to(-LOG2E * jnp.exp(small[6 + n : 7 + n, :]), (GROUP, width))
+    save(rate, rate_out)
+
+    def fetch(source, t, slot):
+        return pltpu.make_async_copy(
+            source.at[:, pl.ds(pl.multiple_of(t * BLOCK, BLOCK), BLOCK), :], stage.at[slot], stage_sems.at[slot]
+        )
+
+    def weave(slot, scaled):
+        for s in range(GROUP):
+            value = stage[slot, s].astype(F32)
+            if scaled:
+                square = jnp.mean(value * value, axis=-1, keepdims=True)
+                value = value * lax.rsqrt(square + EPS)
+            for k in range(held.shape[0]):
+                tile = value[:, k * LANES : (k + 1) * LANES]
+                if scaled:
+                    at = gain_row + k % 2
+                    tile = tile * small[at : at + 1, (k // 2) * LANES : (k // 2 + 1) * LANES]
+                held[k, pl.ds(s, BLOCK, stride=GROUP), :] = tile
+
+    block_rows = BLOCK * GROUP
+    blocks = total // block_rows
+
+    def block_of(t):
+        return pl.ds(pl.multiple_of(t * block_rows, block_rows), block_rows)
+
+    pass_on(0, tokens_all)
+    own_grads = exchange(1, out_grad, grads_all)
+    ring.step(0, 3)
+    exchanged(0, tokens_all, own_tokens)
+    fetch(tokens_all, 0, 0).start()
+
+    @pl.loop(0, blocks)
+    def _(t):
+        slot = lax.rem(t, 2)
+
+        @pl.when(t + 1 < blocks)
+        def _():
+            fetch(tokens_all, t + 1, 1 - slot).start()
+
+        @pl.when(t == blocks - 2)
+        def _():
+            ring.step(0, 4)
+            ring.step(1, 1)
+
+        fetch(tokens_all, t, slot).wait()
+        weave(slot, True)
+        for k in range(held.shape[0]):
+            normed[block_of(t), k * LANES : (k + 1) * LANES] = held[k].astype(BF16)
+
+    save(normed, normed_out)
+    for copy in own_shards:
+        copy.wait()
+    ring.finish(0)
+    save(w_in, w_in_out)
+
+    def cotangent_out_of(t, slot):
+        return pltpu.make_async_copy(cotangent.at[slot], cotangent_out.at[block_of(t), :], out_sems.at[slot])
+
+    def weave_grads(first, count):
+        fetch(grads_all, first, first % 2).start()
+
+        @pl.loop(first, first + count)
+        def _(t):
+            slot = lax.rem(t, 2)
+
+            @pl.when(t + 1 < first + count)
+            def _():
+                fetch(grads_all, t + 1, 1 - slot).start()
+
+            @pl.when(t >= 2)
+            def _():
+                cotangent_out_of(t - 2, slot).wait()
+
+            fetch(grads_all, t, slot).wait()
+            weave(slot, False)
+            for k in range(held.shape[0]):
+                cotangent[slot, :, k * LANES : (k + 1) * LANES] = held[k].astype(BF16)
+            cotangent_out_of(t, slot).start()
+
+    inner[0:pad, :] = jnp.zeros((pad, width), F32)
+    part[...] = jnp.zeros_like(part)
+
+    @pl.loop(0, width // chunk)
+    def _(c):
+        cols = pl.ds(pl.multiple_of(c * chunk, chunk), chunk)
+        inner[pad:, cols] = jnp.dot(normed[...], w_in[:, cols], preferred_element_type=F32)
+
+        @pl.when(c == 1)
+        def _():
+            ring.step(2, 1)
+
+        tap = [small[taps + i : taps + i + 1, cols] for i in range(5)]
+
+        @pl.loop(0, total // rows)
+        def _(i):
+            start = pl.multiple_of(i * rows, rows)
+            value = tap[4] + tap[3] * inner[pl.ds(pad + start, rows), cols]
+            for shift in range(1, 4):
+                mask = tiled(masks[shift - 1, pl.ds(start, rows), :], chunk)
+                before = inner[pl.ds(pad - shift * GROUP + start, rows), cols]
+                value = value + tap[3 - shift] * (before * mask)
+            here = value * sigmoid(value)
+            act[pl.ds(start, rows), cols] = here
+            low[pl.ds(start, rows), cols] = here.astype(BF16)
+
+        for j in range(2):
+            part[j] += lax.dot_general(
+                low[:, cols], few_all[j * LANES : (j + 1) * LANES, cols], (((1,), (1,)), ((), ())),
+                preferred_element_type=F32,
+            )
+
+    save(inner.at[pl.ds(pad, total), :], inner_out)
+    save(act, act_out)
+    save(low, low_out)
+
+    near = (near_send, near_recv)
+    for j in range(2):
+        for s in range(GROUP):
+            nat[j, s * length : (s + 1) * length, :] = part[j, pl.ds(s, length, stride=GROUP), :]
+    sends = []
+
+    def start(source, target, index, peer):
+        copy = remote(source, target, near, index, peer)
+        copy.start()
+        sends.append(copy)
+
+    def come(target, index, peer):
+        remote(target, target, near, index, peer).wait_recv()
+
+    for i in range(2):
+        start(nat.at[:, pl.ds((2 * i + 1) * side_rows, side_rows), :], got_near.at[i], i, peers.core)
+    ring.step(1, 2)
+    pass_on(1, grads_all)
+    for i in range(2):
+        come(got_near.at[i], i, peers.core)
+    to_across[...] = nat[:, 2 * side_rows : 3 * side_rows, :] + got_near[1]
+    start(to_across, got_across, 2, peers.across)
+    exchanged(1, grads_all, own_grads)
+    weave_grads(0, blocks // 2)
+    ring.step(2, 2)
+    come(got_across, 2, peers.across)
+    mine = nat[:, :side_rows, :] + got_near[0] + got_across[...]
+    shared[0, 0] = mine[0].astype(BF16)
+    lane = lax.broadcasted_iota(jnp.int32, (side_rows, LANES), 1)
+    rest, terms = jnp.where(lane < 2 * nstate, mine[1], 0.0), jnp.zeros((side_rows, LANES), F32)
+    for i in range(3):
+        term = rest.astype(BF16).astype(F32)
+        rest = rest - term
+        terms = terms + (pltpu.roll(term, 2 * nstate * i, 1) if i else term)
+    shared[0, 1] = terms.astype(BF16)
+    start(shared.at[0], shared.at[2], 3, peers.across)
+    start(shared.at[0], shared.at[1], 4, peers.core)
+    weave_grads(blocks // 2, blocks // 2)
+    come(shared.at[2], 3, peers.across)
+    start(shared.at[2], shared.at[3], 5, peers.core)
+    come(shared.at[1], 4, peers.core)
+    come(shared.at[3], 5, peers.core)
+    for copy in sends:
+        copy.wait_send()
+    for k in range(COPIES):
+        for b in range(batches):
+            for j in range(2):
+                part[j, pl.ds(k * batches + b, length, stride=GROUP), :] = shared[
+                    k, j, b * length : (b + 1) * length, :
+                ].astype(F32)
+    step_low[...] = part[0].astype(BF16)
+    coef[...] = part[1].astype(BF16)
+    save(step_low, step_low_out)
+    save(coef, coef_out)
+
+    stride = few_all[rank + 2 * nstate : 2 * rank + 2 * nstate, :]
+    side_bias = small[bias_row : bias_row + 1, :]
+    carry[...] = jnp.zeros_like(carry)
+
+    def keep_start(t, slot):
+        return pltpu.make_async_copy(start_at.at[slot], start_out.at[t], start_sems.at[slot])
+
+    @pl.loop(0, blocks)
+    def _(t):
+        for tick, which, number in ((0, 1, 3), (2, 2, 3), (4, 1, 4), (6, 2, 4)):
+
+            @pl.when(t == tick)
+            def _(which=which, number=number):
+                ring.step(which, number)
+
+        base = pl.multiple_of(t * block_rows, block_rows)
+        these = block_of(t)
+        wide[...] = jnp.dot(coef[these, :], spread_by[...], preferred_element_type=F32)
+        pre[...] = jnp.dot(step_low[these, :], stride, preferred_element_type=F32)
+        for i in range(BLOCK // 2):
+            sub = slice(i * 2 * GROUP, (i + 1) * 2 * GROUP)
+            step[pl.ds(base + i * 2 * GROUP, 2 * GROUP), :] = softplus(pre[sub, :] + side_bias)
+        slot = lax.rem(t, 2)
+
+        @pl.when(t >= 2)
+        def _():
+            keep_start(t - 2, slot).wait()
+
+        start_at[slot] = carry[...]
+        keep_start(t, slot).start()
+        for c in range(width // chunk):
+            cols = slice(c * chunk, (c + 1) * chunk)
+
+            def advance(i, states):
+                at = pl.ds(pl.multiple_of(base + i * GROUP, GROUP), GROUP)
+                here = at_time(i)
+                step_t, act_t = step[at, cols], act[at, cols]
+                drive = jnp.where(tiled(masks[0, at, :], chunk) > 0.5, step_t, FAR)
+                inflow = step_t * act_t
+                out = small[skip_row : skip_row + 1, cols] * act_t
+                now = []
+                for n in range(nstate):
+                    write = tiled(wide[here, n * LANES : (n + 1) * LANES], chunk)
+                    read = tiled(wide[here, (nstate + n) * LANES : (nstate + n + 1) * LANES], chunk)
+                    state = jnp.exp2(drive * rate[n, :, cols]) * states[n] + write * inflow
+                    out = out + read * state
+                    now.append(state)
+                readout[at, cols] = out
+                return tuple(now)
+
+            states = lax.fori_loop(
+                0, BLOCK, advance, tuple(carry[n, :, cols] for n in range(nstate)), unroll=4
+            )
+            for n in range(nstate):
+                carry[n, :, cols] = states[n]
+
+    save(step, step_out)
+    save(readout, readout_out)
+
+    ring.finish(1)
+    save(gate_w, gate_w_out)
+
+    def keep_gate(c, slot):
+        cols = pl.ds(pl.multiple_of(c * chunk, chunk), chunk)
+        return pltpu.make_async_copy(gate.at[slot], gate_out.at[:, cols], gate_sems.at[slot])
+
+    @pl.loop(0, width // chunk)
+    def _(c):
+        cols = pl.ds(pl.multiple_of(c * chunk, chunk), chunk)
+        slot = lax.rem(c, 2)
+
+        @pl.when(c >= 2)
+        def _():
+            keep_gate(c - 2, slot).wait()
+
+        gate[slot] = jnp.dot(normed[...], gate_w[:, cols], preferred_element_type=F32)
+        keep_gate(c, slot).start()
+
+        @pl.loop(0, total // rows)
+        def _(i):
+            at = pl.ds(pl.multiple_of(i * rows, rows), rows)
+            here = gate[slot, at, :]
+            value = readout[at, cols] * (here * sigmoid(here))
+            gated[at, cols] = value.astype(BF16)
+            for k in range(chunk // LANES):
+                nat[k, at, :] = value[:, k * LANES : (k + 1) * LANES]
+
+        for k in range(chunk // LANES):
+            for s in range(GROUP):
+                natural[s * length : (s + 1) * length, pl.ds(pl.multiple_of(c * chunk + k * LANES, LANES), LANES)] = nat[
+                    k, pl.ds(s, length, stride=GROUP), :
+                ].astype(BF16)
+
+    save(gated, gated_out)
+    save(natural, natural_out)
+    own[1].wait()
+    ring.finish(2)
+    ring.sent_all()
+    for moving in sent:
+        moving.wait_send()
+    for slot in range(2):
+        keep_start(blocks - 2 + slot, slot).wait()
+        keep_gate(width // chunk - 2 + slot, slot).wait()
+        cotangent_out_of(blocks - 2 + slot, slot).wait()
+    for copy in saved:
+        copy.wait()
+
+
+def forward(size, rank, nstate, entry, few, tokens, out_grad, segments, out_proj):
+    batches, length, model = tokens.shape
+    total = COPIES * batches * length
+    slab, width = entry.shape[0], size * LANES
+    blocks = length // BLOCK
+    anywhere = pl.BlockSpec(memory_space=pl.ANY)
+    half = size // 2
+    dma = pltpu.SemaphoreType.DMA
+    shape = jax.ShapeDtypeStruct
+    full, low = shape((total, width), F32), shape((total, width), BF16)
+    thin = shape((total, LANES), BF16)
+    rows = shape((total, model), BF16)
+    weights = shape((size * slab, width), BF16)
+    few_all = shape((few.shape[0], width), BF16)
+    masks = shape((3, total, LANES), F32)
+    state = shape((nstate, GROUP, width), F32)
+    spread_by = shape((LANES, 2 * nstate * LANES), BF16)
+    fold_by = shape((2 * nstate * LANES, LANES), BF16)
+    outs = dict(
+        few=few_all,
+        masks=masks,
+        rate=state,
+        spread_by=spread_by,
+        fold_by=fold_by,
+        normed=rows,
+        cotangent=rows,
+        tokens_all=shape((GROUP, length, model), BF16),
+        grads_all=shape((GROUP, length, model), BF16),
+        segments_all=shape((COPIES,) + segments.shape, segments.dtype),
+        inner_in=weights,
+        inner=full,
+        act=full,
+        act_low=low,
+        step_low=thin,
+        coef=thin,
+        step=full,
+        starts=shape((blocks,) + state.shape, F32),
+        gate=full,
+        readout=full,
+        gated=low,
+        gated_natural=low,
+        gate_in=weights,
+        out_w=shape((size * out_proj.shape[0] // COPIES, model), BF16),
+    )
+    quarter = total // COPIES
+    scratch = [
+        few_all,
+        shape((few.shape[0] - 2 * rank - 2 * nstate, width), F32),
+        masks,
+        state,
+        spread_by,
+        fold_by,
+        rows,
+        shape((2, GROUP, BLOCK, model), BF16),
+        shape((2, BLOCK * GROUP, model), BF16),
+        shape((model // LANES, BLOCK * GROUP, LANES), F32),
+        shape((COPIES,) + segments.shape, segments.dtype),
+        shape((slab, width), BF16),
+        shape((slab, width), BF16),
+        weights,
+        shape((total + 3 * GROUP, width), F32),
+        full,
+        low,
+        shape((2, total, LANES), F32),
+        shape((2, total, LANES), F32),
+        shape((2, 2, quarter, LANES), F32),
+        shape((2, quarter, LANES), F32),
+        shape((2, quarter, LANES), F32),
+        shape((COPIES, 2, quarter, LANES), BF16),
+        thin,
+        thin,
+        shape((BLOCK * GROUP, 2 * nstate * LANES), F32),
+        shape((BLOCK * GROUP, width), F32),
+        full,
+        full,
+        state,
+        shape((2,) + state.shape, F32),
+        shape((2, total, 256), F32),
+        low,
+        low,
+        weights,
+    ]
+    sems = [(20,), (2,), (2,), (7,), (2 * size,), (2,), (2,), (1,)]
+    sems += [(3, 2, half, 2)] * 2 + [(2, half)] * 2 + [(3, 3)] * 2 + [(6,)] * 2
+    results = pl.pallas_call(
+        functools.partial(forward_kernel, size, rank, nstate),
+        in_specs=[anywhere] * 6,
+        out_specs=[anywhere] * len(outs),
+        out_shape=list(outs.values()),
+        scratch_shapes=[pltpu.VMEM(x.shape, x.dtype) for x in scratch] + [dma(n) for n in sems],
+        compiler_params=pltpu.CompilerParams(
+            collective_id=4, has_side_effects=True, vmem_limit_bytes=62 * 1024 * 1024
+        ),
+        cost_estimate=cost(8 * total * width * model, 100 * total * width),
+        name="forward",
+    )(entry, few, tokens, out_grad, segments, out_proj)
+    return dict(zip(outs, results))
 
 
 class Guests:
@@ -871,11 +1334,11 @@
 
 
 def scan_back_kernel(
-    nstate, chunk, rings, pre_ref, step_ref, act_ref, grad_ref, coef_ref, spread_ref, fold_ref, keep_ref, rate_ref,
+    nstate, chunk, rings, step_ref, act_ref, grad_ref, coef_ref, spread_ref, fold_ref, keep_ref, rate_ref,
     row_ref, start_ref, *refs,
 ):
     wide, states_all, decays, parts, sizes = refs[-5:]
-    width = pre_ref.shape[1]
+    width = step_ref.shape[1]
     step_now = pl.program_id(0)
     if rings:
         first_ref, second_ref = refs[:2]
@@ -963,7 +1426,9 @@
         for n in range(nstate):
             carry_ref[n, :, cols] = carry[n]
 
-    pre_grad = sizes[...] * sigmoid(pre_ref[...] + row_ref[0:1])
+    step = step_ref[...]
+    series = step * (1.0 - step * (0.5 - step * (1.0 / 6.0)))
+    pre_grad = sizes[...] * jnp.where(step < 0.01, series, 1.0 - jnp.exp(-step))
     pre_grad_ref[...] = pre_grad.astype(BF16)
     total = pre_grad[:GROUP]
     for t in range(1, BLOCK):
@@ -982,9 +1447,9 @@
 
 
 def scan_backward(
-    pre, step, act, grad, coef, spread_by, fold_by, keep, rate, rows, starts, rings, wgrads
+    step, act, grad, coef, spread_by, fold_by, keep, rate, rows, starts, rings, wgrads
 ):
-    total, width = pre.shape
+    total, width = step.shape
     nstate = rate.shape[0]
     size = BLOCK * GROUP
     chunk = 256
@@ -1002,7 +1467,6 @@
         functools.partial(scan_back_kernel, nstate, chunk, rings),
         grid=(count,),
         in_specs=[
-            tile,
             tile,
             tile,
             tile,
@@ -1040,7 +1504,7 @@
         else params(),
         cost_estimate=cost(40 * work, 24 * count * size * width),
         name="scan_backward",
-    )(pre, step, act, grad, coef, spread_by, fold_by, keep, rate, rows, starts, *wgrads)
+    )(step, act, grad, coef, spread_by, fold_by, keep, rate, rows, starts, *wgrads)
 
 
 def spread_columns_kernel(copy_ref, *refs):
@@ -1154,9 +1618,10 @@
     few = jnp.pad(few, ((0, -few.shape[0] % 16), (0, 0)))
     small_ring = ring.half == 4
     own = [tokens, out_grad, segment_ids[:, 0, :]]
-    if small_ring and aligned:
-        inner_in, gate_shard, few_all, *copies = gather_all(fsdp, in_proj, few, own)
-        few_all = few_all.astype(F32)
+    fused = small_ring and aligned
+    if fused:
+        out = forward(fsdp, rank, nstate, in_proj, few, *own, out_proj)
+        few_all = out["few"].astype(F32)
     else:
         gathers = [Gather(ring, inner_shard), Gather(ring, few)]
         for gather in gathers:
@@ -1164,11 +1629,8 @@
         inner_in, few_all = (gather.whole for gather in gathers)
         few_all = jnp.moveaxis(few_all, 0, 1).reshape(-1, width).astype(F32)
         copies = [jnp.stack(rep_gather(value)) for value in own]
-    inner_in, out_shard = lax.optimization_barrier((inner_in, mine(out_proj)))
-    gate_gather = Gather(ring, gate_shard)
-    out_gather = Gather(ring, out_shard)
-    inner_in = inner_in.reshape(model, width)
-    values, cotangent, segments = (c.reshape((GROUP,) + c.shape[2:]) for c in copies)
+        inner_in = inner_in.reshape(model, width)
+        values, cotangent, segments = (c.reshape((GROUP,) + c.shape[2:]) for c in copies)
 
     sizes = [rank + 2 * nstate, rank, taps_n, 1, 1, nstate, 1, gains_n]
     pieces, start = [], 0
@@ -1186,83 +1648,43 @@
             masks.append((earlier == segments).astype(F32).T.reshape(total, 1))
         return jnp.broadcast_to(jnp.stack(masks), (taps_n - 1, total, LANES))
 
-    def small_terms():
-        tap_rows = jnp.concatenate(
-            [taps, shift_bias, jnp.zeros((7 - taps_n, width), F32)]
-        )
-        side_rows = jnp.concatenate(
-            [size_bias, skip, jnp.zeros((6, width), F32)]
-        )
-        decay_rate = -jnp.exp(decay)
-        rate = jnp.broadcast_to((decay_rate * LOG2E)[:, None, :], (nstate, GROUP, width))
-        return tap_rows, side_rows, decay_rate, rate, masks_of(segments), spreader(nstate), folder(nstate)
-
-    tap_rows, side_rows, decay_rate, rate, masks, spread_by, fold_by = small_terms()
-    normed = interleave(values, gain)
-    keep = masks[0]
-
-    state0 = jnp.zeros((nstate, GROUP, width), F32)
-    blocks = length // BLOCK
-    store = {}
-
-    def g1():
-        inner = dot(normed, inner_in, 1, 0)
-        return (inner,) + tuple(conv_forward(inner, masks, tap_rows))
-
-    def g2():
-        part_sums = dot(store["act_low"], select, 1, 1)
-        return sum_near(by_copy(part_sums))
-
-    def g3():
-        projected = to_time(sum_far(store["half_sums"]).reshape(total, -1))
-        store["step_low"] = projected[:, :rank].astype(BF16)
-        store["coef"] = spread(projected[:, rank:], nstate)
-        store["pre"] = dot(store["step_low"], stride, 1, 0)
-        return store["step_low"], store["coef"], store["pre"], forward_part(0, (), state0)
-
-    def forward_part(first, before, held):
-        return tuple(
-            scan_forward(
-                store["pre"], store["act"], store["coef"], spread_by, keep, rate, side_rows,
-                held, before, first, blocks // 2,
+    tap_rows = jnp.concatenate([taps, shift_bias, jnp.zeros((7 - taps_n, width), F32)])
+    side_rows = jnp.concatenate([size_bias, skip, jnp.zeros((6, width), F32)])
+    decay_rate = -jnp.exp(decay)
+
+    if fused:
+        (
+            masks, rate, spread_by, fold_by, normed, cotangent, inner_in, inner, act, act_low, step_low, coef, step,
+            starts, gate, readout, gated, gated_natural, gate_in, out_w,
+        ) = (
+            out[k]
+            for k in (
+                "masks", "rate", "spread_by", "fold_by", "normed", "cotangent", "inner_in", "inner", "act", "act_low",
+                "step_low", "coef", "step", "starts", "gate", "readout", "gated", "gated_natural", "gate_in", "out_w",
             )
         )
-
-    def g4():
-        out = store["scan"]
-        return forward_part(blocks // 2, out[:3], out[3])
-
-    movers = [gate_gather] if small_ring else []
-    ((store["inner"], store["act"], store["act_low"]),) = slot(1, movers, g1)
-    (store["half_sums"],) = slot(2, movers, g2)
-    ((store["step_low"], store["coef"], store["pre"], store["scan"]),) = slot(3, movers, g3)
-    (store["scan"],) = slot(4, movers, g4)
-    if not small_ring:
-        gate_gather.rest()
-    readout, step, starts, _ = store["scan"]
-    gate_in = gate_gather.whole.reshape(model, width)
-
-    def o1():
-        return dot(normed, gate_in, 1, 0)
-
-    def o2():
-        return gate_forward(readout, store["gate"])
-
-    def o3():
-        return dot(gated, cotangent, 0, 0).astype(BF16).reshape(fsdp, part, model)
-
-    movers = [out_gather] if small_ring else []
-    (store["gate"],) = slot(1, movers, o1)
-    (gated, gated_natural), cotangent = slot(2, movers, o2, lambda: interleave(cotangent))
-    (out_wgrad,) = slot(3, movers, o3)
-    slot(4, movers)
-    if not small_ring:
-        out_gather.rest()
-    out_w = out_gather.whole.reshape(width, model)
-    gate, inner, act, act_low = (store[k] for k in ("gate", "inner", "act", "act_low"))
-    pre, coef, step_low = store["pre"], store["coef"], store["step_low"]
-
-    fused = small_ring and aligned
+    else:
+        rate = jnp.broadcast_to((decay_rate * LOG2E)[:, None, :], (nstate, GROUP, width))
+        masks, spread_by, fold_by = masks_of(segments), spreader(nstate), folder(nstate)
+        normed, cotangent = interleave(values, gain), interleave(cotangent)
+        gathers = [Gather(ring, gate_shard), Gather(ring, mine(out_proj))]
+        for gather in gathers:
+            gather.rest()
+        gate_in = gathers[0].whole.reshape(model, width)
+        out_w = gathers[1].whole.reshape(width, model)
+        inner = dot(normed, inner_in, 1, 0)
+        act, act_low = conv_forward(inner, masks, tap_rows)
+        half_sums = sum_near(by_copy(to_sequence(dot(act_low, select, 1, 1))))
+        projected = to_time(sum_far(half_sums).reshape(total, -1))
+        step_low = projected[:, :rank].astype(BF16)
+        coef = spread(projected[:, rank:], nstate)
+        pre = dot(step_low, stride, 1, 0)
+        readout, step, starts = scan_forward(pre, act, coef, spread_by, masks[0], rate, side_rows)
+        gate = dot(normed, gate_in, 1, 0)
+        gated, gated_natural = gate_forward(readout, gate)
+    keep = masks[0]
+    out_wgrad = dot(gated, cotangent, 0, 0).astype(BF16).reshape(fsdp, part, model)
+
     def r1():
         return gate_backward(dot(cotangent, out_w, 1, 1), readout, gate)
 
@@ -1271,7 +1693,7 @@
     gate_wgrad = dot(normed, gate_grad, 0, 0).astype(BF16).reshape(fsdp, slab, width)
     wgrads = [out_wgrad, gate_wgrad] if fused else []
     pre_low, direct, coef_part, _, sums, *totals = scan_backward(
-        pre, step, act, read_grad, coef, spread_by, fold_by, keep, rate, side_rows, starts,
+        step, act, read_grad, coef, spread_by, fold_by, keep, rate, side_rows, starts,
         fsdp if fused else 0, wgrads,
     )
     if not fused:
@@ -1297,13 +1719,13 @@
     )
 
     def conv_part():
-        proj_low = sum_far(half_sums).reshape(total, -1).astype(BF16)
-        act_grad = direct + dot(to_time(proj_low), select, 1, 0)
+        proj_time = to_time(sum_far(half_sums).reshape(total, -1).astype(BF16))
+        act_grad = direct + dot(proj_time, select, 1, 0)
         inner_grad, inner_grad_natural, conv_sums = conv_backward(inner, act_grad, masks, tap_rows)
         inner_wgrad = dot(normed, inner_grad, 0, 0).astype(BF16).reshape(fsdp, slab, width)
         small = jnp.concatenate(
             [
-                dot(proj_low, act_low, 0, 0),
+                dot(proj_time, act_low, 0, 0),
                 dot(step_low, pre_low, 0, 0),
                 conv_sums[: taps_n + 1],
                 jnp.sum(sums[nstate + 1 :], axis=1),

time: 623 us -> 498 us (0.80)
  local copies, waits for them, and re-layouts: 60.4 us -> 28.7 us
  between operations: 25.5 us -> 1.6 us
  starting transfers between devices: 26.7 us -> 3.65 us
  waiting for transfers between devices: 28.1 us -> 7.72 us
  matrix products: 86 us -> 67.7 us
  other arithmetic: 36.1 us -> 24.9 us
    dynamic_update_slice x18 -> x0, local copies, waits for them, and re-layouts: 22 us -> none  [put(): self.whole = lax.dynamic_update_slice(self.whole, piece[None], at)]
    dot_general x15 -> x11, matrix products: 86 us -> 67.7 us  [dot(): lax.dot_general(left, right, (((left_dim,), (right_dim,)), ((), ())), pre...]
    ppermute x16 -> x0, starting transfers between devices: 18.1 us -> none  [the longest x8 15 us: up(): return lax.ppermute(value, 'fsdp', self.above)]
    ppermute x14 -> x11, waiting for transfers between devices: 17.9 us -> 7.72 us  [swap(): return lax.ppermute(value, 'rep', [(r, r ^ bit) for r in range(COPIES)])]
    ppermute x16 -> x0, waiting for transfers between devices: 10.2 us -> none  [the longest x8 5.61 us: up(): return lax.ppermute(value, 'fsdp', self.above)]
    convert_element_type x5 -> x1, other arithmetic: 7.4 us -> 0.13 us  [on_device(): few_all = out['few'].astype(F32)]
    pallas_call x9 -> x1, Pallas kernels: 151 us -> 150 us  [forward(): pl.pallas_call(functools.partial(forward_kernel, size, rank, nstate), in_...]
  transfers between devices with their start and end apart: 30 -> 11, of which waited for: 9 -> 1; matrix products, arithmetic and copies ran while one was open for 21% -> 16% of each run, Pallas kernels for 16% -> 20%
where the time goes in v1:
time: 498 us; the launch traced here: 488 us
  Pallas kernels  353 us (71%)
  matrix products  67.7 us (14%)
  local copies, waits for them, and re-layouts  28.7 us (6%)
  other arithmetic  24.9 us (5%)
  waiting for transfers between devices  7.72 us (2%)
    pallas_call x1, Pallas kernels, forward(): pl.pallas_call(functools.partial(forward_kernel, size, rank, nstate), in_...  150 us
    pallas_call x1, Pallas kernels, scan_backward(): pl.pallas_call(functools.partial(scan_back_kernel, nstate, chunk, rings),...  95.8 us
    dot_general x11, matrix products, dot(): lax.dot_general(left, right, (((left_dim,), (right_dim,)), ((), ())), pre...  67.7 us
    pallas_call x1, Pallas kernels, scatter_all(): pl.pallas_call(functools.partial(scatter_kernel, size), in_specs=[inside]...  63.6 us
    pallas_call x1, Pallas kernels, conv_backward(): pl.pallas_call(conv_back_kernel, grid=(width // LANES,), in_specs=[tile,...  14.3 us
    pallas_call x2, Pallas kernels, spread_columns(): pl.pallas_call(spread_columns_kernel, grid_spec=pltpu.PrefetchScalarGridS...  13.8 us
    pallas_call x1, Pallas kernels, gate_backward(): pl.pallas_call(gate_back_kernel, grid=(width // LANES,), in_specs=[tile]...  11.3 us
  transfers between devices with their start and end apart: 11, of which 1 were waited for; matrix products, arithmetic and copies ran while one was open for 16% of the time, Pallas kernels for 20%

profile of v1, /device:TPU:0, one launch (start us, length us, event | category | flops | bytes accessed | tf_op | source)
XLA Modules:
  0.0 487.7 jit_solution(418659602345145480)
XLA Ops:
  0.7 0.8 dynamic-slice_bitcast_fusion.5
  1.5 0.7 dynamic-slice_bitcast_fusion.2
  2.1 0.7 dynamic-slice_bitcast_fusion.1
  2.8 0.8 constant_dynamic-slice_fusion
  3.7 0.8 dynamic-slice_bitcast_fusion.3
  4.5 0.9 concatenate.16
  5.5 0.6 pad.10.few
  6.1 150.4 %forward.1 = (bf16[320,1024]{1,0:T(8,128)(2,1)}, f32[3,1024,128]{2,1,0:T(8,128)}, f32[16,8,1024]{2,1,0:T(8,128)}, bf16[128,4096]{1,0:T(8,128)(2,1)}, bf16[4096,1...) custom-call(bf16[256,8192]{1,0:T(8,128)(2,1)} %refs_4_.3, ...), custom_call_target="tpu_custom_call" | custom-call | flops 17179869184 | bytes 104857600 | tf_op jit(solution)/shard_map/forward/pallas_call | solution.py:1265
  156.5 0.7 fusion.19
  157.2 1.9 slice_bitcast_fusion.4.keep_ref
  159.1 9.5 %convolution_convert_fusion.3 = bf16[1024,2048]{1,0:T(8,128)(2,1)} fusion(bf16[1024,1024]{1,0:T(8,128)(2,1)} %get-tuple-element.81, bf16[1024,2048]{1,0:T(8,128)(2,1)} %get-tuple-element.69), kind=kOutput, calls=%fused_computation.5 | convolution fusion | flops 4297064448 | bytes 10485760 | tf_op jit(solution)/shard_map/dot_general | solution.py:24
  168.6 6.5 %fusion.23.grad_ref = f32[1024,1024]{1,0:T(8,128)} fusion(bf16[1024,2048]{1,0:T(8,128)(2,1)S(1)} %copy-done.19, bf16[1024,2048]{1,0:T(8,128)(2,1)S(1)} %copy-done.21), kind=kOutput, calls=%fused_computation.78 | convolution fusion | flops 4294967296 | bytes 12582912 | tf_op jit(solution)/shard_map/dot_general | solution.py:24
  175.2 11.3 %gate_backward.1 = (f32[1024,1024]{1,0:T(8,128)}, bf16[1024,1024]{1,0:T(8,128)(2,1)}, bf16[1024,1024]{1,0:T(8,128)(2,1)}) custom-call(f32[1024,1024]{1,0:T(8,128)} %fusion.23.grad_ref, f32[1024,1024]{1,0:T(8,128)} %get-tuple-element.71.readout_ref, f32[1024,1024]{1,0:T(8,128)} %get-tuple-element.72.gate_ref), custom_call_target="tpu_custom_call" | custom-call | flops 20971520 | bytes 20971520 | tf_op jit(solution)/shard_map/gate_backward/pallas_call | solution.py:338
  186.6 7.7 %convolution_convert_fusion.2 = bf16[2048,1024]{1,0:T(8,128)(2,1)} fusion(bf16[1024,2048]{1,0:T(8,128)(2,1)S(1)} %copy-done.22, bf16[1024,1024]{1,0:T(8,128)(2,1)} %get-tuple-element.83), kind=kOutput, calls=%fused_computation.4 | convolution fusion | flops 4297064448 | bytes 10485760 | tf_op jit(solution)/shard_map/dot_general | solution.py:24
  194.3 0.7 maximum_maximum_fusion.row_ref
  195.0 95.8 %scan_backward.1 = (bf16[1024,1024]{1,0:T(8,128)(2,1)}, f32[1024,1024]{1,0:T(8,128)}, f32[1024,128]{1,0:T(8,128)}, f32[16,8,1024]{2,1,0:T(8,128)}, f32[18,8,1024...) custom-call(f32[1024,1024]{1,0:T(8,128)} %get-tuple-element.67.step_ref, ...), custom_call_target="tpu_custom_call" | custom-call | flops 671088640 | bytes 25165824 | tf_op jit(solution)/shard_map/scan_backward/pallas_call | solution.py:1466
  291.0 1.9 collective-permute-start.9
  293.2 1.2 copy.41
  294.4 2.4 fusion.10
  296.9 0.3 copy.42
  297.2 0.4 fusion.17
  298.2 0.7 pad_maximum_fusion.2
  299.4 0.8 slice_reduce_fusion.1
  300.2 1.2 slice_reduce_fusion
  301.3 8.3 %convolution_convert_fusion.1 = bf16[1024,2048]{1,0:T(8,128)(2,1)} fusion(bf16[1024,1024]{1,0:T(8,128)(2,1)S(1)} %copy-done.23, bf16[1024,2048]{1,0:T(8,128)(2,1)} %get-tuple-element.70), kind=kOutput, calls=%fused_computation.3 | convolution fusion | flops 4297064448 | bytes 10485760 | tf_op jit(solution)/shard_map/dot_general | solution.py:24
  310.2 10.7 %fusion.24 = f32[1024,2048]{1,0:T(8,128)} fusion(bf16[1024,1024]{1,0:T(8,128)(2,1)} %get-tuple-element.90, bf16[2048,1024]{1,0:T(8,128)(2,1)} %get-tuple-element.91), kind=kOutput, calls=%fused_computation.79 | convolution fusion | flops 4294967296 | bytes 14680064 | tf_op jit(solution)/shard_map/dot_general | solution.py:24
  321.3 0.6 concatenate.19.taps_ref
  322.1 0.4 copy-done.2
  322.5 0.5 convolution_convert_fusion.5
  323.3 7.7 %collective-permute-done.1 = f32[2,256,160]{1,2,0:T(8,128)S(1)} collective-permute-done((f32[2,256,160]{1,2,0:T(8,128)S(1)}, f32[2,256,160]{1,2,0:T(8,128)S(1)}, u32[]{:S(2)}, u32[]{:S(2)}) %collective-permute-start.1) | collective-permute-done | bytes 327712 | tf_op jit(solution)/shard_map/ppermute | solution.py:164
  331.4 0.5 copy-done.14
  331.9 1.5 pad_maximum_fusion
  333.4 4.2 spread_rows.1
  337.7 0.8 copy-done.13
  338.5 6.9 %spread_columns.2 = (f32[256,8192]{1,0:T(8,128)}, f32[256,128]{1,0:T(8,128)}) custom-call(s32[1]{0:T(128)} %bitcast.28.copy_ref, bf16[256,1024]{1,0:T(8,128)(2,1)} %get-tuple-element.110.refs_0_, bf16[256,1024]{1,0:T(8,128)(2,1)} %collective-permute-done.8.refs_1_, bf16[256,1024]{1,0:T(8,128)(2,1)} %collective-permute-done.9.refs_2_, ...), custom_call_target="tpu_custom_call" | custom-call | flops 1048576 | bytes 5242880 | tf_op jit(solution)/shard_map/spread_columns/pallas_call | solution.py:1534
  345.8 0.5 copy.48
  346.3 4.9 %convolution_add_fusion.grad_ref = f32[1024,1024]{1,0:T(8,128)} fusion(f32[1024,1024]{1,0:T(8,128)} %get-tuple-element.84, bf16[128,8,160]{2,1,0:T(8,128)(2,1)S(1)} %copy.48, bf16[320,1024]{1,0:T(8,128)(2,1)S(1)} %copy-done.8), kind=kOutput, calls=%fused_computation.10 | convolution fusion | flops 336592896 | bytes 9240576 | tf_op jit(solution)/shard_map/dot_general | solution.py:24
  351.2 14.3 %conv_backward.1 = (bf16[1024,1024]{1,0:T(8,128)(2,1)}, bf16[1024,1024]{1,0:T(8,128)(2,1)}, f32[8,1024]{1,0:T(8,128)}) custom-call(f32[1024,1024]{1,0:T(8,128)} %get-tuple-element.66.inner_ref, f32[1024,1024]{1,0:T(8,128)} %convolution_add_fusion.grad_ref, f32[3,1024,128]{2,1,0:T(8,128)} %get-tuple-element.77.masks_ref, f32[8,1024]{1,0:T(8,128)} %concatenate.19.taps_ref), custom_call_target="tpu_custom_call" | custom-call | flops 62914560 | bytes 10485760 | tf_op jit(solution)/shard_map/conv_backward/pallas_call | solution.py:286
  365.6 0.8 slice.263
  366.3 0.5 convolution_convert_fusion.4
  366.9 0.5 concatenate.20
  367.4 1.0 bitcast_bitcast_fusion.small_ref
  368.4 9.5 %convolution_convert_fusion = bf16[2048,1024]{1,0:T(8,128)(2,1)} fusion(bf16[1024,2048]{1,0:T(8,128)(2,1)} %get-tuple-element.82, bf16[1024,1024]{1,0:T(8,128)(2,1)} %get-tuple-element.95), kind=kOutput, calls=%fused_computation.2 | convolution fusion | flops 4297064448 | bytes 10485760 | tf_op jit(solution)/shard_map/dot_general | solution.py:24
  377.9 3.4 fusion.6
  381.3 0.3 collective-permute-start.7
  381.6 7.1 %fusion.25 = f32[1024,2048]{1,0:T(8,128)} fusion(bf16[1024,1024]{1,0:T(8,128)(2,1)S(1)} %copy-done.18, bf16[2048,1024]{1,0:T(8,128)(2,1)S(1)} %copy-done.20), kind=kOutput, calls=%fused_computation.80 | convolution fusion | flops 4294967296 | bytes 14680064 | tf_op jit(solution)/shard_map/dot_general | solution.py:24
  388.7 9.2 %add_convert_fusion = bf16[1024,2048]{1,0:T(8,128)(2,1)} fusion(f32[1024,2048]{1,0:T(8,128)} %fusion.25, f32[1024,2048]{1,0:T(8,128)} %fusion.24), kind=kLoop, calls=%fused_computation.1 | loop fusion | flops 4194304 | bytes 20971520 | tf_op jit(solution)/shard_map/convert_element_type | solution.py:1746
  397.9 63.6 %scatter_all.1 = (bf16[4,256,1024]{2,1,0:T(8,128)(2,1)}, bf16[4,320,128]{2,1,0:T(8,128)(2,1)}, f32[256,2048]{1,0:T(8,128)}) custom-call(bf16[8,256,1024]{2,1,0:T(8,128)(2,1)} %bitcast.121, bf16[8,320,128]{2,1,0:T(8,128)(2,1)} %bitcast_bitcast_fusion.small_ref, bf16[4,256,2048]{2,1,0:T(8,128)(2,1)} %bitcast.116), custom_call_target="tpu_custom_call" | custom-call | bytes 8388608 | tf_op jit(solution)/shard_map/scatter_all/pallas_call | solution.py:543
  461.5 3.1 slice_bitcast_fusion
  464.6 0.6 fusion.1
  465.2 2.3 gather_fusion
  467.4 1.0 convert_bitcast_fusion
  468.5 0.8 copy-done.9
  469.3 0.7 slice.232
  470.0 1.8 copy.52
  471.8 6.9 %spread_columns.3 = (f32[256,8192]{1,0:T(8,128)}, f32[256,128]{1,0:T(8,128)}) custom-call(s32[1]{0:T(128)} %bitcast.28.copy_ref, bf16[256,1024]{1,0:T(8,128)(2,1)} %get-tuple-element.131.refs_0_, bf16[256,1024]{1,0:T(8,128)(2,1)} %get-tuple-element.130.refs_1_, bf16[256,1024]{1,0:T(8,128)(2,1)} %get-tuple-element.129.refs_2_, ...), custom_call_target="tpu_custom_call", output_to_operand_aliasing={{0}: (6, {})} | custom-call | flops 1048576 | bytes 5242880 | tf_op jit(solution)/shard_map/spread_columns/pallas_call | solution.py:1534
  478.7 1.0 add_reduce_fusion
  479.8 0.6 convert_divide_fusion
  480.4 0.6 fusion.18
  480.9 0.6 slice_bitcast_fusion.7
  481.5 0.6 bitcast_bitcast_fusion.2
  482.2 0.8 bitcast_bitcast_fusion.1
  482.9 1.6 convert_add_fusion.1
  485.1 2.1 fusion.4
  (96 shorter events, 4.5 us)
Async XLA Ops:
  0.6 3.1 copy-start
  159.1 9.5 %copy-start.19 = (bf16[1024,2048]{1,0:T(8,128)(2,1)S(1)}, bf16[1024,2048]{1,0:T(8,128)(2,1)}, u32[]{:S(2)}) copy-start(bf16[1024,2048]{1,0:T(8,128)(2,1)} %get-tuple-element.69) | copy-start | bytes 12582916
  159.1 9.5 %copy-start.21 = (bf16[1024,2048]{1,0:T(8,128)(2,1)S(1)}, bf16[1024,2048]{1,0:T(8,128)(2,1)}, u32[]{:S(2)}) copy-start(bf16[1024,2048]{1,0:T(8,128)(2,1)} %get-tuple-element.70) | copy-start | bytes 12582916
  175.2 11.4 %copy-start.22 = (bf16[1024,2048]{1,0:T(8,128)(2,1)S(1)}, bf16[1024,2048]{1,0:T(8,128)(2,1)}, u32[]{:S(2)}) copy-start(bf16[1024,2048]{1,0:T(8,128)(2,1)} %get-tuple-element.82) | copy-start | bytes 12582916
  195.0 99.4 %copy-start.8 = (bf16[320,1024]{1,0:T(8,128)(2,1)S(1)}, bf16[320,1024]{1,0:T(8,128)(2,1)}, u32[]{:S(2)}) copy-start(bf16[320,1024]{1,0:T(8,128)(2,1)} %get-tuple-element.79) | copy-start | bytes 1966084
  290.8 31.1 %collective-permute-start.3 = (bf16[128,2048]{1,0:T(8,128)(2,1)}, bf16[128,2048]{1,0:T(8,128)(2,1)}, u32[]{:S(2)}, u32[]{:S(2)}) collective-permute-start(bf16[128,2048]{1,0:T(8,128)(2,1)} %get-tuple-element.116.refs_0_), channel_id=1, source_target_pairs={{0,2},{1,3},{2,0},{3,1},{4,6},{5,7},{6,4},{7,5},{8,10},{9,11},{10,... | collective-permute-start | bytes 1572872 | tf_op jit(solution)/shard_map/ppermute | solution.py:164
  290.9 40.1 %collective-permute-start.2 = (bf16[128,2048]{1,0:T(8,128)(2,1)}, bf16[128,2048]{1,0:T(8,128)(2,1)}, u32[]{:S(2)}, u32[]{:S(2)}) collective-permute-start(bf16[128,2048]{1,0:T(8,128)(2,1)} %get-tuple-element.116.refs_0_), channel_id=1, source_target_pairs={{0,1},{1,0},{2,3},{3,2},{4,5},{5,4},{6,7},{7,6},{8,9},{9,8},{10,11... | collective-permute-start | bytes 1572872 | tf_op jit(solution)/shard_map/ppermute | solution.py:164
  291.0 32.0 %collective-permute-start.9 = (bf16[256,1024]{1,0:T(8,128)(2,1)}, bf16[256,1024]{1,0:T(8,128)(2,1)}, u32[]{:S(2)}, u32[]{:S(2)}) collective-permute-start(bf16[256,1024]{1,0:T(8,128)(2,1)} %get-tuple-element.110.refs_0_), channel_id=1, source_target_pairs={{0,2},{1,3},{2,0},{3,1},{4,6},{5,7},{6,4},{7,5},{8,10},{9,11},{10,... | collective-permute-start | bytes 1572872 | tf_op jit(solution)/shard_map/ppermute | solution.py:164
  292.9 44.8 %collective-permute-start.8 = (bf16[256,1024]{1,0:T(8,128)(2,1)}, bf16[256,1024]{1,0:T(8,128)(2,1)}, u32[]{:S(2)}, u32[]{:S(2)}) collective-permute-start(bf16[256,1024]{1,0:T(8,128)(2,1)} %get-tuple-element.110.refs_0_), channel_id=1, source_target_pairs={{0,1},{1,0},{2,3},{3,2},{4,5},{5,4},{6,7},{7,6},{8,9},{9,8},{10,11... | collective-permute-start | bytes 1572872 | tf_op jit(solution)/shard_map/ppermute | solution.py:164
  298.2 3.2 copy-start.23
  298.9 22.0 %collective-permute-start = (f32[2,256,160]{1,2,0:T(8,128)}, f32[2,256,160]{1,2,0:T(8,128)S(1)}, u32[]{:S(2)}, u32[]{:S(2)}) collective-permute-start(f32[2,256,160]{1,2,0:T(8,128)} %pad_maximum_fusion.2), channel_id=1, source_target_pairs={{0,1},{1,0},{2,3},{3,2},{4,5},{5,4},{6,7},{7,6},{8,9},{9,8},{10,11... | collective-permute-start | bytes 983048 | tf_op jit(solution)/shard_map/ppermute | solution.py:164
  310.2 11.9 %copy-start.15 = (bf16[1024,128]{1,0:T(8,128)(2,1)S(1)}, bf16[1024,128]{1,0:T(8,128)(2,1)}, u32[]{:S(2)}) copy-start(bf16[1024,128]{1,0:T(8,128)(2,1)} %get-tuple-element.97) | copy-start | bytes 786436
  320.9 1.6 copy-start.2
  321.0 10.1 %copy-start.5 = (bf16[1024,2048]{1,0:T(8,128)(2,1)S(1)}, bf16[1024,2048]{1,0:T(8,128)(2,1)}, u32[]{:S(2)}) copy-start(bf16[1024,2048]{1,0:T(8,128)(2,1)} %convolution_convert_fusion.1) | copy-start | bytes 12582916
  321.1 9.9 %collective-permute-start.1 = (f32[2,256,160]{1,2,0:T(8,128)S(1)}, f32[2,256,160]{1,2,0:T(8,128)S(1)}, u32[]{:S(2)}, u32[]{:S(2)}) collective-permute-start(f32[2,256,160]{1,2,0:T(8,128)S(1)} %pad_maximum_fusion.3), channel_id=1, source_target_pairs={{0,2},{1,3},{2,0},{3,1},{4,6},{5,7},{6,4},{7,5},{8,10},{9,11},{10,... | collective-permute-start | bytes 983048 | tf_op jit(solution)/shard_map/ppermute | solution.py:164
  322.0 9.1 %collective-permute-start.4 = (bf16[128,2048]{1,0:T(8,128)(2,1)}, bf16[128,2048]{1,0:T(8,128)(2,1)S(1)}, u32[]{:S(2)}, u32[]{:S(2)}) collective-permute-start(bf16[128,2048]{1,0:T(8,128)(2,1)} %collective-permute-done.3.refs_2_), channel_id=1, source_target_pairs={{0,1},{1,0},{2,3},{3,2},{4,5},{5,4},{6,7},{7,6},{8,9},{9,8},{10,11... | collective-permute-start | bytes 1572872 | tf_op jit(solution)/shard_map/ppermute | solution.py:164
  323.0 14.7 %collective-permute-start.10 = (bf16[256,1024]{1,0:T(8,128)(2,1)}, bf16[256,1024]{1,0:T(8,128)(2,1)S(1)}, u32[]{:S(2)}, u32[]{:S(2)}) collective-permute-start(bf16[256,1024]{1,0:T(8,128)(2,1)} %collective-permute-done.9.refs_2_), channel_id=1, source_target_pairs={{0,1},{1,0},{2,3},{3,2},{4,5},{5,4},{6,7},{7,6},{8,9},{9,8},{10,11... | collective-permute-start | bytes 1572872 | tf_op jit(solution)/shard_map/ppermute | solution.py:164
  331.1 0.8 copy-start.14
  331.1 14.3 %collective-permute-start.5 = (bf16[2,256,160]{1,2,0:T(8,128)(2,1)S(1)}, bf16[2,256,160]{1,2,0:T(8,128)(2,1)S(1)}, u32[]{:S(2)}, u32[]{:S(2)}) collective-permute-start(bf16[2,256,160]{1,2,0:T(8,128)(2,1)S(1)} %fusion.44), channel_id=1, source_target_pairs={{0,1},{1,0},{2,3},{3,2},{4,5},{5,4},{6,7},{7,6},{8,9},{9,8},{10,11... | collective-permute-start | bytes 491528 | tf_op jit(solution)/shard_map/ppermute | solution.py:164
  333.4 44.5 %collective-permute-start.6 = (bf16[2,256,2048]{2,1,0:T(8,128)(2,1)}, bf16[2,256,2048]{2,1,0:T(8,128)(2,1)}, u32[]{:S(2)}, u32[]{:S(2)}) collective-permute-start(bf16[2,256,2048]{2,1,0:T(8,128)(2,1)} %pad_maximum_fusion), channel_id=1, source_target_pairs={{0,1},{1,0},{2,3},{3,2},{4,5},{5,4},{6,7},{7,6},{8,9},{9,8},{10,11... | collective-permute-start | bytes 6291464 | tf_op jit(solution)/shard_map/ppermute | solution.py:164
  337.7 0.8 copy-start.13
  351.2 15.1 %copy-start.11 = (bf16[1024,1024]{1,0:T(8,128)(2,1)S(1)}, bf16[1024,1024]{1,0:T(8,128)(2,1)}, u32[]{:S(2)}) copy-start(bf16[1024,1024]{1,0:T(8,128)(2,1)} %get-tuple-element.96) | copy-start | bytes 6291460
  368.4 9.6 %copy-start.6 = (bf16[1024,2048]{1,0:T(8,128)(2,1)S(1)}, bf16[1024,2048]{1,0:T(8,128)(2,1)}, u32[]{:S(2)}) copy-start(bf16[1024,2048]{1,0:T(8,128)(2,1)} %convolution_convert_fusion.1) | copy-start | bytes 12582916
  377.9 3.7 copy-start.18
  377.9 3.7 copy-start.20
  381.3 101.6 %collective-permute-start.7 = (bf16[256,2048]{1,0:T(8,128)(2,1)}, bf16[256,2048]{1,0:T(8,128)(2,1)}, u32[]{:S(2)}, u32[]{:S(2)}) collective-permute-start(bf16[256,2048]{1,0:T(8,128)(2,1)} %get-tuple-element.102), channel_id=1, source_target_pairs={{0,2},{1,3},{2,0},{3,1},{4,6},{5,7},{6,4},{7,5},{8,10},{9,11},{10,... | collective-permute-start | bytes 3145736 | tf_op jit(solution)/shard_map/ppermute | solution.py:164
  461.5 3.1 copy-start.3
  461.5 3.1 copy-start.7
  468.5 0.8 copy-start.9
  471.8 6.9 %copy-start.16 = (f32[256,128]{1,0:T(8,128)S(1)}, f32[256,128]{1,0:T(8,128)}, u32[]{:S(2)}) copy-start(f32[256,128]{1,0:T(8,128)} %get-tuple-element.113) | copy-start | bytes 393220
  471.8 8.0 %copy-start.17 = (bf16[256]{0:T(256)(128)(2,1)S(1)}, bf16[256]{0:T(256)(128)(2,1)}, u32[]{:S(2)}) copy-start(bf16[256]{0:T(256)(128)(2,1)} %param.16) | copy-start | bytes 1540
  471.8 8.5 %copy-start.10 = (f32[320,4,128]{2,0,1:T(8,128)S(1)}, f32[320,4,128]{2,0,1:T(8,128)}, u32[]{:S(2)}) copy-start(f32[320,4,128]{2,0,1:T(8,128)} %copy-done.9) | copy-start | bytes 1966084
  482.9 1.9 copy-start.4
  482.9 2.2 copy-start.12
  485.1 2.1 copy-start.1
